TPU v7x, 32 devices: a whole 2x2x4 slice. The times are simulated.
32 devices in a mesh: basin: 2 (over x), pair: 8 (over z, y), row: 2 (over core).
Axes of the slice: x: 2, y: 2, z: 4, core: 2. Of those that a mesh axis runs over, the one named last changes fastest.
Arguments:
- snapshots: float32 [8192, 4096], P(('basin', 'row'), 'pair'), parts along dimension 0, may hold values from -60 to 60, as said below
- plan: int32 [4, 16], replicated, may hold values from 0 to 15, as said below
Outputs:
- rotated: float32 [8192, 4096], P(('basin', 'row'), 'pair'), parts along dimension 0
There are 2 independent parts, one for each index of `basin`. A program takes and returns all parts, laid end to end along the dimension named above; an argument that names none is the same for every part. Nothing has to cross between parts.
Inputs may be any that keep to these rules, and one draw needn't show every extreme that they name: `plan`: each row of the table is a permutation of the 16 slots. Slots 2d and 2d + 1 lie on the d-th index of pair; in every round each index sends one of its two blocks to index d + 1 and the other to index d - 1 (both modulo 8). `snapshots`: real values.
All inputs are finite; a program needn't handle non-finite values.
Results may differ from a plain program's by a relative error of at most 0.0003.
Values sent between devices are 32-bit elements; how exact they have to be, the bound alone decides.
No kernel may reach another device: no remote copies, remote signals or barrier semaphores. Data moves between devices by JAX's collectives and lax.ppermute only.
A program may use at most 64 MiB of HBM per device.

v0:
```python
import functools

import jax
import jax.numpy as jnp
from jax import lax
from jax.experimental import pallas as pl
from jax.experimental.pallas import tpu as pltpu
from jax.sharding import PartitionSpec as P

NS_ITERS = 6
EPSILON = 1e-06
BLOCK = 256
PIECES = 4
SIDE = 128
PUT = 64
FIRST_MIB = 48
PARAMS = pltpu.CompilerParams(vmem_limit_bytes=12 * 1024 * 1024)
LARGE = pltpu.CompilerParams(vmem_limit_bytes=24 * 1024 * 1024)
FIRST = pltpu.CompilerParams(vmem_limit_bytes=FIRST_MIB * 1024 * 1024)


def shift(value, axis, by):
    size = lax.axis_size(axis)
    return lax.ppermute(value, axis, [(i, (i + by) % size) for i in range(size)])


def split(value):
    high = value.astype(jnp.bfloat16)
    return high, (value - high.astype(jnp.float32)).astype(jnp.bfloat16)


def dot(left, right):
    return jnp.dot(left, right, preferred_element_type=jnp.float32)


def dot3(left, right):
    (left_high, left_low), (right_high, right_low) = left, right
    return dot(left_high, right_high) + dot(left_low, right_high) + dot(left_high, right_low)


def whole(shape):
    return pl.BlockSpec(shape, lambda *_: (0,) * len(shape))


SMEM = pl.BlockSpec(memory_space=pltpu.SMEM)


COST = pl.CostEstimate(flops=1024, bytes_accessed=1024, transcendentals=0)
LONG = pl.CostEstimate(flops=4_000_000_000, bytes_accessed=1024, transcendentals=0)


def eye(size):
    row = lax.broadcasted_iota(jnp.int32, (size, size), 0)
    column = lax.broadcasted_iota(jnp.int32, (size, size), 1)
    return jnp.where(row == column, 1.0, 0.0).astype(jnp.float32)


def route(count, plan, device):
    stay_first = jnp.int32(1)
    flags = []
    for step in range(plan.shape[0]):
        odd = step % 2
        position = lax.rem(device + odd, count)
        upper = lax.rem(position + 1, count)
        second = 2 * position + 1
        second_up = jnp.where((plan[step, 2 * upper] == second) | (plan[step, 2 * upper + 1] == second), 1, 0)
        send_second = second_up if odd else 1 - second_up
        flags.append((stay_first, jnp.where(send_second == stay_first, 0, 1)))
        target = device if odd else upper
        below = lax.rem(target + count - 1, count)
        from_below = jnp.where(plan[step, 2 * target] // 2 == below, 1, 0)
        stay_first = 1 - from_below if odd else from_below
    return flags, stay_first


def flags_kernel(count, plan, device, flags):
    rounds = plan.shape[0]
    own, stay_first = route(count, plan, device[0])
    above, _ = route(count, plan, lax.rem(device[0] + 2, count))
    below, _ = route(count, plan, lax.rem(device[0] + count - 2 % count, count))
    for step in range(rounds):
        flags[step, 0], flags[step, 1] = own[step]
        sender = below[step] if step % 2 else above[step]
        flags[rounds + step, 0] = 1 - sender[0]
        flags[rounds + step, 1] = 1 - sender[1]
    flags[2 * rounds, 0] = 1 - stay_first
    flags[2 * rounds, 1] = stay_first
    flags[2 * rounds + 1, 0] = device[1]
    flags[2 * rounds + 1, 1] = device[1]


def make_flags(plan, device, count):
    return pl.pallas_call(
        functools.partial(flags_kernel, count),
        in_specs=[SMEM, SMEM],
        out_specs=SMEM,
        out_shape=jax.ShapeDtypeStruct((2 * plan.shape[0] + 2, 2), jnp.int32),
        compiler_params=PARAMS,
        cost_estimate=COST,
        name="flags",
    )(plan, device)


def column(row):
    return jnp.broadcast_to(row, (SIDE, row.shape[1])).T


def row_sums(value):
    return jnp.sum((value * value).reshape(-1, 8, value.shape[1]), axis=0)


def first_gram_kernel(snapshots, total, norm, held, done):
    rows, columns = snapshots.shape
    width = columns // 2

    def read(index):
        rows = pl.ds(pl.multiple_of(index * BLOCK, BLOCK), BLOCK)
        return pltpu.make_async_copy(snapshots.at[rows], held.at[index], done.at[index])

    for index in range(rows // BLOCK):
        read(index).start()
    total[...] = jnp.zeros_like(total)

    def step(index, squares):
        read(index).wait()
        kept = held[index, :, :width]
        add_gram(total, kept.T, held[index, :, width:])
        return squares + row_sums(kept)

    squares = lax.fori_loop(0, rows // BLOCK, step, jnp.zeros((8, width), jnp.float32))
    norm[...] = column(jnp.sum(squares, axis=0, keepdims=True))


def first_gram(snapshots):
    rows, columns = snapshots.shape
    width = columns // 2
    vmem = pl.BlockSpec(memory_space=pltpu.VMEM)
    blocks = rows // BLOCK
    return pl.pallas_call(
        first_gram_kernel,
        in_specs=[pl.BlockSpec(memory_space=pl.ANY)],
        out_specs=[vmem, vmem],
        out_shape=[
            jax.ShapeDtypeStruct((width + 8, width), jnp.float32),
            jax.ShapeDtypeStruct((width, SIDE), jnp.float32),
        ],
        scratch_shapes=[pltpu.VMEM((blocks, BLOCK, columns), jnp.float32), pltpu.SemaphoreType.DMA((blocks,))],
        compiler_params=pltpu.CompilerParams(vmem_limit_bytes=52 * 1024 * 1024),
        cost_estimate=COST,
        name="first_gram",
    )(snapshots)


def add_gram(total, turned, value):
    width = value.shape[1]
    total[:width, :] += dot3(split(turned), split(value))
    total[width:, :] += row_sums(value)


def over_blocks(lists, body, carry=None, skip=None):
    skip = skip or [0] * len(lists)
    cuts, ends = [], []
    for pieces, first in zip(lists, skip):
        start, cut = -first, []
        for ref, turned in pieces:
            size = ref.shape[1] if turned else ref.shape[0]
            cut.append((start, start + size, ref, turned))
            start += size
        cuts.append(cut)
        ends.append(start)
    marks = sorted({max(0, edge) for cut in cuts for piece in cut for edge in piece[:2] if edge <= min(ends)})
    for low, high in zip(marks, marks[1:]):
        found = [next(piece for piece in cut if piece[0] <= low < piece[1]) for cut in cuts]

        def step(index, carry):
            views = []
            for start, _, ref, turned in found:
                rows = pl.ds(pl.multiple_of(low - start + index * BLOCK, BLOCK), BLOCK)
                views.append(ref.at[:, rows] if turned else ref.at[rows])
            return body(views, carry)

        carry = lax.fori_loop(0, (high - low) // BLOCK, step, carry)
    return carry


def straight(refs):
    return [(ref, False) for ref in refs]


def transposed(refs):
    return [(ref, True) for ref in refs]


def gram_kernel(counts, offset, *refs):
    turned, refs = refs[: counts[0]], refs[counts[0] :]
    came, refs = refs[: counts[1]], refs[counts[1] :]
    total = refs[-1]
    total[...] = refs[0][...] if counts[2] else jnp.zeros_like(total)

    def body(views, carry):
        add_gram(total, views[0][...], views[1][...])
        return carry

    over_blocks((transposed(turned), straight(came)), body, 0, (offset * BLOCK, 0))


def gram(turned, came, before=(), after=(), offset=0):
    width = came[0].shape[1]
    vmem = pl.BlockSpec(memory_space=pltpu.VMEM)
    args = (*turned, *came, *before)
    return pl.pallas_call(
        functools.partial(gram_kernel, (len(turned), len(came), len(before)), offset),
        in_specs=[vmem] * len(args) + [pl.BlockSpec(memory_space=pl.ANY)] * len(after),
        out_specs=vmem,
        out_shape=jax.ShapeDtypeStruct((width + 8, width), jnp.float32),
        compiler_params=PARAMS,
        cost_estimate=COST,
        name="gram",
    )(*args, *after)


def rotation_kernel(step, side, both, note, piece, flags, mine, other, norm, *refs):
    width = mine.shape[1]
    *refs, base, inverse = refs
    if piece:
        snapshots, *refs, held, done = refs
        copy = pltpu.make_async_copy(snapshots.at[pl.ds(0, held.shape[0])], held, done)
        copy.start()
    first_core = flags[flags.shape[0] - 1, 0] == 0
    if note == "read":
        one, two = mine[: width // 2, :], other[: width // 2, :]
        total = jnp.concatenate((jnp.where(first_core, one, two), jnp.where(first_core, two, one)), axis=0)
        norm_move = mine[width // 2 : width // 2 + 1, :]
        norm_stay = column(mine[width // 2 + 1 : width // 2 + 2, :])[:, :1]
    else:
        total = mine[...] + other[...]
        norm_move = jnp.sum(total[width:, :], axis=0, keepdims=True)
        norm_stay = norm[:, side : side + 1]
        total = total[:width, :]
    if note == "write":
        *refs, message = refs
        message[: width // 2, :] = jnp.where(first_core, total[: width // 2, :], total[width // 2 :, :])
        stay_row = norm[:, side : side + SIDE].T[:1, :]
        index = lax.broadcasted_iota(jnp.int32, (8, width), 0)
        message[width // 2 :, :] = jnp.where(index == 0, norm_move, stay_row)
    coupled = total / (norm_stay + norm_move + EPSILON)
    turned = coupled.T
    stay_first = flags[step, 0] == (0 if note == "read" else 1)
    send_is_stay = flags[step, 1] == (0 if note == "read" else 1)
    coupling = jnp.where(stay_first, coupled, turned)
    coupling_turned = jnp.where(stay_first, turned, coupled)
    identity = eye(width)
    scale = 1.0 / (1.0 + jnp.sum(coupled * coupled))
    left, right = split(coupling_turned), split(coupling)
    base[...] = scale * (identity + dot3(right, left))
    inverse[...] = scale * identity

    def sweep(_, carry):
        pair = split(base[...])
        inverse[...] = 2.0 * inverse[...] - dot3(split(inverse[...]), pair)
        base[...] = 2.0 * base[...] - dot3(pair, pair)
        return carry

    lax.fori_loop(0, NS_ITERS, sweep, 0)
    inverse = inverse[...]
    product_turned = dot3(left, split(inverse))
    second_second = identity - 2.0 * dot3(split(product_turned), right)
    first_first = 2.0 * inverse - identity
    first_second = 2.0 * product_turned.T
    second_first = -2.0 * product_turned
    stay_stay = jnp.where(stay_first, first_first, second_second)
    move_move = jnp.where(stay_first, second_second, first_first)
    stay_move = jnp.where(stay_first, first_second, second_first)
    move_stay = jnp.where(stay_first, second_first, first_second)
    top = split(jnp.where(send_is_stay, stay_stay, stay_move))
    end = split(jnp.where(send_is_stay, move_stay, move_move))
    if len(refs) > 2:
        *refs, sent = refs
        copy.wait()
        sent[...] = dot3(split(held[:, :width]), top) + dot3(split(held[:, width:]), end)
    high, low = refs
    for ref, upper, lower in zip((high, low), top, end):
        ref[:width, :width] = upper
        ref[width:, :width] = lower
    if both:
        top = split(jnp.where(send_is_stay, stay_move, stay_stay))
        end = split(jnp.where(send_is_stay, move_move, move_stay))
        for ref, upper, lower in zip((high, low), top, end):
            ref[:width, width:] = upper
            ref[width:, width:] = lower


def rotation(step, side, both, flags, total, norm, note=None, snapshots=(), size=0):
    other = shift(total, "row", 1)
    width = total.shape[1]
    matrix = (2 * width, 2 * width if both else width)
    shapes = [(size, width)] if snapshots else [(width // 2 + 8, width)] if note == "write" else []
    return pl.pallas_call(
        functools.partial(rotation_kernel, step, side, both, note, bool(snapshots)),
        grid=(1,),
        in_specs=[SMEM, whole(total.shape), whole(other.shape), whole(norm.shape)]
        + [pl.BlockSpec(memory_space=pl.ANY)] * len(snapshots),
        out_specs=[whole(matrix)] * 2 + [whole(shape) for shape in shapes],
        out_shape=[jax.ShapeDtypeStruct(matrix, jnp.bfloat16)] * 2
        + [jax.ShapeDtypeStruct(shape, jnp.float32) for shape in shapes],
        scratch_shapes=([pltpu.VMEM((size, 2 * width), jnp.float32), pltpu.SemaphoreType.DMA] if snapshots else [])
        + [pltpu.VMEM((width, width), jnp.float32)] * 2,
        compiler_params=FIRST if snapshots else PARAMS,
        cost_estimate=LONG if note == "read" else COST,
        name="rotation",
    )(flags, total, other, norm, *snapshots)


def apply_both_kernel(first, joined, high, low, *refs):
    if not first:
        before, *refs = refs
    sent, sent_turned, kept, kept_turned, norm = refs
    width = sent.shape[1]
    result = dot3(split(joined[...]), (high[...], low[...]))
    sent[...] = result[:, :width]
    kept[...] = result[:, width:]
    squares = []
    for half, ref in ((result[:, width:], kept_turned), (result[:, :width], sent_turned)):
        turned = half.T
        ref[...] = turned
        squares.append(jnp.broadcast_to(jnp.sum(turned * turned, axis=1, keepdims=True), (width, SIDE)))
    squares = jnp.concatenate(squares, axis=1)
    step = pl.program_id(0)

    @pl.when(step == 0)
    def _():
        norm[...] = squares if first else before[...] + squares

    @pl.when(step > 0)
    def _():
        norm[...] += squares


def apply_both(snapshots, start, high, low, before, blocks):
    width = high.shape[0] // 2
    rows = blocks * BLOCK
    block = (BLOCK, width)
    by_row = pl.BlockSpec(block, lambda i: (i, 0))
    by_column = pl.BlockSpec((width, BLOCK), lambda i: (0, i))
    norm = whole((width, 2 * SIDE))
    piece = jax.ShapeDtypeStruct((rows, width), jnp.float32)
    turned = jax.ShapeDtypeStruct((width, rows), jnp.float32)
    first = before is None
    return pl.pallas_call(
        functools.partial(apply_both_kernel, first),
        grid=(blocks,),
        in_specs=[pl.BlockSpec((BLOCK, 2 * width), lambda i: (start + i, 0)), whole(high.shape), whole(low.shape)]
        + [norm] * (not first),
        out_specs=[by_row, by_column, by_row, by_column, norm],
        out_shape=[piece, turned, piece, turned, jax.ShapeDtypeStruct((width, 2 * SIDE), jnp.float32)],
        compiler_params=FIRST,
        cost_estimate=COST,
        name="apply_both",
    )(snapshots, high, low, *([] if first else [before]))


def rotate(one, two, high, low):
    joined = jnp.concatenate((one[...], two[...]), axis=1)
    return dot3(split(joined), (high[...], low[...]))


def apply_all_kernel(counts, *refs):
    stay, refs = refs[: counts[0]], refs[counts[0] :]
    move, refs = refs[: counts[1]], refs[counts[1] :]
    high, low, sent, sent_turned, kept_turned, norm, *kept = refs
    width = norm.shape[0]

    def body(views, sums):
        one, two, sent, sent_turned, kept, kept_turned = views
        result = rotate(one, two, high, low)
        new = []
        for start, ref, turned, total in ((width, kept, kept_turned, sums[0]), (0, sent, sent_turned, sums[1])):
            value = result[:, start : start + width]
            ref[...] = value
            turned[...] = value.T
            new.append(total + row_sums(value))
        return tuple(new)

    lists = (
        straight(stay),
        straight(move),
        straight([sent]),
        transposed([sent_turned]),
        straight(kept),
        transposed([kept_turned]),
    )
    sums = over_blocks(lists, body, (jnp.zeros((8, width), jnp.float32),) * 2)
    for half in range(2):
        norm[:, half * SIDE : (half + 1) * SIDE] = column(jnp.sum(sums[half], axis=0, keepdims=True))


def apply_all(stay, move, high, low, sizes):
    width = high.shape[0] // 2
    rows = sum(sizes)
    shapes = [(rows, width), (width, rows), (width, rows), (width, 2 * SIDE)] + [(size, width) for size in sizes]
    vmem = pl.BlockSpec(memory_space=pltpu.VMEM)
    sent, sent_turned, kept_turned, norm, *kept = pl.pallas_call(
        functools.partial(apply_all_kernel, (len(stay), len(move))),
        in_specs=[vmem] * (len(stay) + len(move) + 2),
        out_specs=[vmem] * len(shapes),
        out_shape=[jax.ShapeDtypeStruct(shape, jnp.float32) for shape in shapes],
        compiler_params=LARGE,
        cost_estimate=COST,
        name="apply_all",
    )(*stay, *move, high, low)
    return sent, sent_turned, kept, kept_turned, norm


def rebuild_kernel(counts, *refs):
    sent, refs = refs[: counts[0]], refs[counts[0] :]
    raw, refs = refs[: counts[1]], refs[counts[1] :]
    high, low, turned, came, total = refs
    total[...] = jnp.zeros_like(total)

    def body(views, carry):
        one, two, kept, out = views
        value = rotate(one, two, high, low)
        out[...] = value
        add_gram(total, kept[...], value)
        return carry

    over_blocks((straight(sent), straight(raw), transposed([turned]), straight([came])), body, 0)


def rebuild(sent, raw, high, low, turned):
    width, rows = turned.shape
    vmem = pl.BlockSpec(memory_space=pltpu.VMEM)
    args = (*sent, *raw, high, low, turned)
    return pl.pallas_call(
        functools.partial(rebuild_kernel, (len(sent), len(raw))),
        in_specs=[vmem] * len(args),
        out_specs=[vmem] * 2,
        out_shape=[
            jax.ShapeDtypeStruct((rows, width), jnp.float32),
            jax.ShapeDtypeStruct((width + 8, width), jnp.float32),
        ],
        compiler_params=LARGE,
        cost_estimate=COST,
        name="rebuild",
    )(*args)


def finish_kernel(counts, kept, aliased, flags, *refs):
    stay, refs = refs[: counts[0]], refs[counts[0] :]
    move, refs = refs[: counts[1]], refs[counts[1] :]
    high, low, *refs = refs
    out, token, held, done = refs[aliased:]
    width = held.shape[1]
    token[...] = jnp.zeros_like(token)
    half = pl.ds(width, width) if kept else pl.ds(0, width)
    column_of = flags[flags.shape[0] - 2, 1 - kept]
    columns = pl.ds(pl.multiple_of(column_of * width, width), width)

    def write(index):
        rows = pl.ds(pl.multiple_of(index * BLOCK, BLOCK), BLOCK)
        return pltpu.make_async_copy(held.at[rows], out.at[rows, columns], done.at[index])

    def body(views, index):
        one, two, block = views
        block[...] = rotate(one, two, high.at[:, half], low.at[:, half])
        write(index).start()
        return index + 1

    over_blocks((straight(stay), straight(move), straight([held])), body, 0)
    for index in range(min(sum(ref.shape[0] for ref in pieces) for pieces in (stay, move)) // BLOCK):
        write(index).wait()


def put_kernel(start, flags, came, before, out, done):
    width = came.shape[1]
    columns = pl.ds(pl.multiple_of(flags[flags.shape[0] - 2, 1] * width, width), width)
    copies = []
    for index in range(came.shape[0] // PUT):
        rows = pl.ds(index * PUT, PUT)
        copy = pltpu.make_async_copy(came.at[rows], out.at[pl.ds(start + index * PUT, PUT), columns], done.at[index])
        copy.start()
        copies.append(copy)
    for copy in copies:
        copy.wait()


def put(flags, came, before, start):
    vmem = pl.BlockSpec(memory_space=pltpu.VMEM)
    anywhere = pl.BlockSpec(memory_space=pl.ANY)
    return pl.pallas_call(
        functools.partial(put_kernel, start),
        in_specs=[SMEM, vmem, anywhere],
        out_specs=anywhere,
        out_shape=jax.ShapeDtypeStruct(before.shape, jnp.float32),
        input_output_aliases={2: 0},
        scratch_shapes=[pltpu.SemaphoreType.DMA((came.shape[0] // PUT,))],
        compiler_params=PARAMS,
        cost_estimate=COST,
        name="put",
    )(flags, came, before)


def relay_kernel(message, *refs):
    refs[-1][...] = message[...]


def relay(message, after):
    vmem = pl.BlockSpec(memory_space=pltpu.VMEM)
    return pl.pallas_call(
        relay_kernel,
        in_specs=[vmem] + [pl.BlockSpec(memory_space=pl.ANY)] * len(after),
        out_specs=vmem,
        out_shape=jax.ShapeDtypeStruct(message.shape, jnp.float32),
        compiler_params=PARAMS,
        cost_estimate=COST,
        name="relay",
    )(message, *after)


def apply_one_kernel(skip, stay, move, high, low, sent):
    half = pl.ds(0, sent.shape[1])

    def body(views, carry):
        one, two, out = views
        out[...] = rotate(one, two, high.at[:, half], low.at[:, half])
        return carry

    over_blocks((straight([stay]), straight([move]), straight([sent])), body, 0, (0, skip * BLOCK, 0))


def apply_one(stay, move, high, low, skip):
    vmem = pl.BlockSpec(memory_space=pltpu.VMEM)
    return pl.pallas_call(
        functools.partial(apply_one_kernel, skip),
        in_specs=[vmem] * 4,
        out_specs=vmem,
        out_shape=jax.ShapeDtypeStruct(stay.shape, jnp.float32),
        compiler_params=PARAMS,
        cost_estimate=COST,
        name="apply_one",
    )(stay, move, high, low)


def finish(kept, flags, stay, move, high, low, before, shape, after=()):
    width = high.shape[0] // 2
    vmem = pl.BlockSpec(memory_space=pltpu.VMEM)
    anywhere = pl.BlockSpec(memory_space=pl.ANY)
    args = (flags, *stay, *move, high, low)
    blocks = shape[0] // BLOCK
    return pl.pallas_call(
        functools.partial(finish_kernel, (len(stay), len(move)), kept, len(before) + len(after)),
        in_specs=[SMEM] + [vmem] * (len(args) - 1) + [anywhere] * (len(before) + len(after)),
        out_specs=[anywhere, vmem],
        out_shape=[jax.ShapeDtypeStruct(shape, jnp.float32), jax.ShapeDtypeStruct((8, SIDE), jnp.float32)],
        input_output_aliases={len(args): 0} if before else {},
        scratch_shapes=[pltpu.VMEM((shape[0], width), jnp.float32), pltpu.SemaphoreType.DMA((blocks,))],
        compiler_params=LARGE,
        cost_estimate=COST,
        name="finish",
    )(*args, *before, *after)


def per_device(snapshots, plan):
    rows = snapshots.shape[0]
    rounds = plan.shape[0]
    size = rows // BLOCK // PIECES
    device = lax.axis_index("pair")
    count = lax.axis_size("pair")
    total, norm = first_gram(snapshots)
    flags = make_flags(plan, jnp.stack((device, lax.axis_index("row"))), count)
    norm = norm + shift(norm, "row", 1)
    high, low, outgoing = rotation(0, 0, True, flags, total, norm, None, (snapshots,), size * BLOCK)
    move = [shift(outgoing, "pair", -2)]
    norm = None
    held = [None] * PIECES
    for piece in [*range(1, PIECES), 0]:
        *held[piece], norm = apply_both(snapshots, piece * size, high, low, norm, size)
        if piece:
            move.append(shift(held[piece][0], "pair", -2))
    sent, sent_turned, stay, stay_turned = zip(*held)
    total = ()
    for one, two in zip(stay_turned, move):
        total = (gram((one,), (two,), total),)
    (total,) = total
    for step in range(1, rounds):
        last = step == rounds - 1
        direction = 2 if step % 2 else -2
        raw = [shift(value, "pair", direction) for value in (stay[:-1] if last else stay)]
        norm = norm + shift(norm, "row", 1)
        if last:
            break
        high, low = rotation(step, 0, True, flags, total, norm)
        sizes = [rows // 2, rows // 4, rows // 4] if step == rounds - 2 else [rows // 2] * 2
        new_sent, new_sent_turned, stay, stay_turned, own_norm = apply_all(stay, move, high, low, sizes)
        total = gram(sent_turned, raw, (), (own_norm,))
        high, low = rotation(rounds + step, SIDE, False, flags, total, norm)
        came, total = rebuild(sent, raw, high, low, stay_turned)
        move, norm = (came,), own_norm
        sent, sent_turned = (new_sent,), (new_sent_turned,)
    high, low, message = rotation(step, 0, True, flags, total, norm, note="write")
    message = shift(message, "pair", direction)
    outgoing = apply_one(stay[-1], came, high, low, (rows - stay[-1].shape[0]) // BLOCK)
    last_piece = shift(outgoing, "pair", direction)
    field, token = finish(1, flags, stay, move, high, low, (), snapshots.shape)
    message = relay(message, (outgoing, token, *raw))
    high, low = rotation(rounds + step, SIDE, False, flags, message, norm, note="read")
    field, _ = finish(0, flags, raw, sent, high, low, (field,), snapshots.shape)
    return put(flags, last_piece, field, rows - last_piece.shape[0])


def solution(mesh):
    in_specs = (P(("basin", "row"), "pair"), P())
    out_specs = P(("basin", "row"), "pair")
    return jax.shard_map(
        per_device, mesh=mesh, in_specs=in_specs, out_specs=out_specs, check_vma=False
    )
```

profile of v0, /device:TPU:0, one launch (start us, length us, event | category | flops | bytes accessed | tf_op | source)
XLA Modules:
  0.0 201.6 jit_solution(6060752050766388820)
XLA Ops:
  0.0 3.9 %first_gram.1 = (f32[264,256]{1,0:T(8,128)S(1)}, f32[256,128]{1,0:T(8,128)S(1)}) custom-call(f32[2048,512]{1,0:T(8,128)} %joined.7), custom_call_target="tpu_custom_call" | custom-call | flops 1024 | bytes 1024 | tf_op jit(solution)/shard_map/first_gram/pallas_call | solution.py:139
  4.6 1.4 flags.1
  6.1 4.9 %rotation.7 = (bf16[512,512]{1,0:T(8,128)(2,1)S(1)}, bf16[512,512]{1,0:T(8,128)(2,1)S(1)}, f32[512,256]{1,0:T(8,128)S(1)}) custom-call(s32[10,2]{1,0:T(8,128)S(1)} %flags.1, f32[264,256]{1,0:T(8,128)S(1)} %get-tuple-element.62.mine, f32[264,256]{1,0:T(8,128)S(1)} %collective-permute-done.other, f32[256,128]{1,0:T(8,128)S(1)} %add.12.norm, f32[2048,512]{1,0:T(8,128)} %joined.7), custom_call_target="tpu_custom_call" | custom-call | flops 1024 | bytes 1024 | tf_op jit(solution)/shard_map/rotation/pallas_call | solution.py:298
  10.9 5.1 %collective-permute-start.2 = (f32[512,256]{1,0:T(8,128)S(1)}, f32[512,256]{1,0:T(8,128)S(1)}, u32[]{:S(2)}, u32[]{:S(2)}) collective-permute-start(f32[512,256]{1,0:T(8,128)S(1)} %get-tuple-element.73), channel_id=1, source_target_pairs={{0,12},{2,14},{4,0},{6,2},{8,4},{10,6},{12,8},{14,10},{1,13},{3,15... | collective-permute-start | bytes 1572872 | tf_op jit(solution)/shard_map/ppermute | solution.py:24
  16.0 2.8 %apply_both.4 = (f32[512,256]{1,0:T(8,128)S(1)}, f32[256,512]{1,0:T(8,128)S(1)}, f32[512,256]{1,0:T(8,128)S(1)}, f32[256,512]{1,0:T(8,128)S(1)}, f32[256,256]{1,0:T(8,128)S(1)}) custom-call(f32[2048,512]{1,0:T(8,128)} %joined.7, bf16[512,512]{1,0:T(8,128)(2,1)S(1)} %get-tuple-element.64.high, bf16[512,512]{1,0:T(8,128)(2,1)S(1)} %get-tuple-element.65.low), custom_call_target="tpu_custom_call" | custom-call | flops 1024 | bytes 1024 | tf_op jit(solution)/shard_map/apply_both/pallas_call | solution.py:349
  19.3 2.9 %apply_both.5 = (f32[512,256]{1,0:T(8,128)S(1)}, f32[256,512]{1,0:T(8,128)S(1)}, f32[512,256]{1,0:T(8,128)S(1)}, f32[256,512]{1,0:T(8,128)S(1)}, f32[256,256]{1,0:T(8,128)S(1)}) custom-call(f32[2048,512]{1,0:T(8,128)} %joined.7, bf16[512,512]{1,0:T(8,128)(2,1)S(1)} %get-tuple-element.64.high, bf16[512,512]{1,0:T(8,128)(2,1)S(1)} %get-tuple-element.65.low, ...), custom_call_target="tpu_custom_call" | custom-call | flops 1024 | bytes 1024 | tf_op jit(solution)/shard_map/apply_both/pallas_call | solution.py:349
  22.7 2.9 %apply_both.6 = (f32[512,256]{1,0:T(8,128)S(1)}, f32[256,512]{1,0:T(8,128)S(1)}, f32[512,256]{1,0:T(8,128)S(1)}, f32[256,512]{1,0:T(8,128)S(1)}, f32[256,256]{1,0:T(8,128)S(1)}) custom-call(f32[2048,512]{1,0:T(8,128)} %joined.7, bf16[512,512]{1,0:T(8,128)(2,1)S(1)} %get-tuple-element.64.high, bf16[512,512]{1,0:T(8,128)(2,1)S(1)} %get-tuple-element.65.low, ...), custom_call_target="tpu_custom_call" | custom-call | flops 1024 | bytes 1024 | tf_op jit(solution)/shard_map/apply_both/pallas_call | solution.py:349
  25.7 2.8 %apply_both.7 = (f32[512,256]{1,0:T(8,128)S(1)}, f32[256,512]{1,0:T(8,128)S(1)}, f32[512,256]{1,0:T(8,128)S(1)}, f32[256,512]{1,0:T(8,128)S(1)}, f32[256,256]{1,0:T(8,128)S(1)}) custom-call(f32[2048,512]{1,0:T(8,128)} %joined.7, bf16[512,512]{1,0:T(8,128)(2,1)S(1)} %get-tuple-element.64.high, bf16[512,512]{1,0:T(8,128)(2,1)S(1)} %get-tuple-element.65.low, ...), custom_call_target="tpu_custom_call" | custom-call | flops 1024 | bytes 1024 | tf_op jit(solution)/shard_map/apply_both/pallas_call | solution.py:349
  28.6 2.1 %collective-permute-start.8 = (f32[512,256]{1,0:T(8,128)S(1)}, f32[512,256]{1,0:T(8,128)S(1)}, u32[]{:S(2)}, u32[]{:S(2)}) collective-permute-start(f32[512,256]{1,0:T(8,128)S(1)} %get-tuple-element.69.refs_0_), channel_id=1, source_target_pairs={{0,4},{2,6},{4,8},{6,10},{8,12},{10,14},{12,0},{14,2},{1,5},{3,7},... | collective-permute-start | bytes 1572872 | tf_op jit(solution)/shard_map/ppermute | solution.py:24
  30.7 8.9 %collective-permute-done.3.refs_1_.refs_5_ = f32[512,256]{1,0:T(8,128)S(1)} collective-permute-done((f32[512,256]{1,0:T(8,128)S(1)}, f32[512,256]{1,0:T(8,128)S(1)}, u32[]{:S(2)}, u32[]{:S(2)}) %collective-permute-start.3) | collective-permute-done | bytes 524320 | tf_op jit(solution)/shard_map/ppermute | solution.py:24
  40.0 10.8 %collective-permute-done.4.refs_1_.refs_6_ = f32[512,256]{1,0:T(8,128)S(1)} collective-permute-done((f32[512,256]{1,0:T(8,128)S(1)}, f32[512,256]{1,0:T(8,128)S(1)}, u32[]{:S(2)}, u32[]{:S(2)}) %collective-permute-start.4) | collective-permute-done | bytes 524320 | tf_op jit(solution)/shard_map/ppermute | solution.py:24
  51.2 10.8 %collective-permute-done.5.refs_1_.refs_7_ = f32[512,256]{1,0:T(8,128)S(1)} collective-permute-done((f32[512,256]{1,0:T(8,128)S(1)}, f32[512,256]{1,0:T(8,128)S(1)}, u32[]{:S(2)}, u32[]{:S(2)}) %collective-permute-start.5) | collective-permute-done | bytes 524320 | tf_op jit(solution)/shard_map/ppermute | solution.py:24
  62.6 0.6 gram.7.refs_2_
  63.8 0.6 gram.9.mine
  64.5 1.5 collective-permute-done.6.other
  66.0 4.1 %rotation.8 = (bf16[512,512]{1,0:T(8,128)(2,1)S(1)}, bf16[512,512]{1,0:T(8,128)(2,1)S(1)}) custom-call(s32[10,2]{1,0:T(8,128)S(1)} %flags.1, f32[264,256]{1,0:T(8,128)S(1)} %gram.9.mine, f32[264,256]{1,0:T(8,128)S(1)} %collective-permute-done.6.other, f32[256,256]{1,0:T(8,128)S(1)} %add.13.norm), custom_call_target="tpu_custom_call" | custom-call | flops 1024 | bytes 1024 | tf_op jit(solution)/shard_map/rotation/pallas_call | solution.py:298
  70.2 5.8 %apply_all.2 = (f32[2048,256]{1,0:T(8,128)S(1)}, f32[256,2048]{1,0:T(8,128)S(1)}, f32[256,2048]{1,0:T(8,128)S(1)}, f32[256,256]{1,0:T(8,128)S(1)}, f32[1024,256]{1,0:T(8,128)S(1)}, /*index=5*/f32[1024,256]{1,0:T(8,128)S(1)}) custom-call(f32[512,256]{1,0:T(8,128)S(1)} %get-tuple-element.69.refs_0_, f32[512,256]{1,0:T(8,128)S(1)} %get-tuple-element.70.refs_1_, ...), custom_call_target="tpu_custom_call" | custom-call | flops 1024 | bytes 1024 | tf_op jit(solution)/shard_map/apply_all/pallas_call | solution.py:402
  76.0 4.3 %collective-permute-start.15 = (f32[1024,256]{1,0:T(8,128)S(1)}, f32[1024,256]{1,0:T(8,128)S(1)}, u32[]{:S(2)}, u32[]{:S(2)}) collective-permute-start(f32[1024,256]{1,0:T(8,128)S(1)} %get-tuple-element.84.refs_0_), channel_id=1, source_target_pairs={{0,12},{2,14},{4,0},{6,2},{8,4},{10,6},{12,8},{14,10},{1,13},{3,15... | collective-permute-start | bytes 3145736 | tf_op jit(solution)/shard_map/ppermute | solution.py:24
  80.3 2.0 %collective-permute-start.16 = (f32[1024,256]{1,0:T(8,128)S(1)}, f32[1024,256]{1,0:T(8,128)S(1)}, u32[]{:S(2)}, u32[]{:S(2)}) collective-permute-start(f32[1024,256]{1,0:T(8,128)S(1)} %get-tuple-element.85.refs_1_), channel_id=1, source_target_pairs={{0,12},{2,14},{4,0},{6,2},{8,4},{10,6},{12,8},{14,10},{1,13},{3,15... | collective-permute-start | bytes 3145736 | tf_op jit(solution)/shard_map/ppermute | solution.py:24
  82.3 3.2 %collective-permute-done.11.refs_7_ = f32[512,256]{1,0:T(8,128)S(1)} collective-permute-done((f32[512,256]{1,0:T(8,128)S(1)}, f32[512,256]{1,0:T(8,128)S(1)}, u32[]{:S(2)}, u32[]{:S(2)}) %collective-permute-start.11) | collective-permute-done | bytes 524320 | tf_op jit(solution)/shard_map/ppermute | solution.py:24
  85.6 11.2 %collective-permute-done.10.refs_6_ = f32[512,256]{1,0:T(8,128)S(1)} collective-permute-done((f32[512,256]{1,0:T(8,128)S(1)}, f32[512,256]{1,0:T(8,128)S(1)}, u32[]{:S(2)}, u32[]{:S(2)}) %collective-permute-start.10) | collective-permute-done | bytes 524320 | tf_op jit(solution)/shard_map/ppermute | solution.py:24
  96.8 11.1 %collective-permute-done.9.refs_5_ = f32[512,256]{1,0:T(8,128)S(1)} collective-permute-done((f32[512,256]{1,0:T(8,128)S(1)}, f32[512,256]{1,0:T(8,128)S(1)}, u32[]{:S(2)}, u32[]{:S(2)}) %collective-permute-start.9) | collective-permute-done | bytes 524320 | tf_op jit(solution)/shard_map/ppermute | solution.py:24
  107.9 2.2 %gram.10.mine = f32[264,256]{1,0:T(8,128)S(1)} custom-call(f32[256,512]{1,0:T(8,128)S(1)} %get-tuple-element.87.refs_0_, f32[256,512]{1,0:T(8,128)S(1)} %get-tuple-element.88.refs_1_, f32[256,512]{1,0:T(8,128)S(1)} %get-tuple-element.89.refs_2_, f32[256,512]{1,0:T(8,128)S(1)} %get-tuple-element.90.refs_3_, f32[512,256]{1,0:T(8,128)S(1)} %collective-permute-done.8.refs_4_, ...), custom_call_target="tpu_custom_call" | custom-call | flops 1024 | bytes 1024 | tf_op jit(solution)/shard_map/gram/pallas_call | solution.py:211
  110.3 1.5 collective-permute-done.12.other
  111.8 4.1 %rotation.9 = (bf16[512,256]{1,0:T(8,128)(2,1)S(1)}, bf16[512,256]{1,0:T(8,128)(2,1)S(1)}) custom-call(s32[10,2]{1,0:T(8,128)S(1)} %flags.1, f32[264,256]{1,0:T(8,128)S(1)} %gram.10.mine, f32[264,256]{1,0:T(8,128)S(1)} %collective-permute-done.12.other, f32[256,256]{1,0:T(8,128)S(1)} %add.13.norm), custom_call_target="tpu_custom_call" | custom-call | flops 1024 | bytes 1024 | tf_op jit(solution)/shard_map/rotation/pallas_call | solution.py:298
  115.9 6.3 %rebuild.2 = (f32[2048,256]{1,0:T(8,128)S(1)}, f32[264,256]{1,0:T(8,128)S(1)}) custom-call(f32[512,256]{1,0:T(8,128)S(1)} %get-tuple-element.86.refs_0_, f32[512,256]{1,0:T(8,128)S(1)} %get-tuple-element.74.refs_1_, f32[512,256]{1,0:T(8,128)S(1)} %get-tuple-element.75.refs_2_, f32[512,256]{1,0:T(8,128)S(1)} %get-tuple-element.76.refs_3_, ...), custom_call_target="tpu_custom_call" | custom-call | flops 1024 | bytes 1024 | tf_op jit(solution)/shard_map/rebuild/pallas_call | solution.py:434
  122.8 1.4 collective-permute-done.14
  124.3 4.2 %rotation.10 = (bf16[512,512]{1,0:T(8,128)(2,1)S(1)}, bf16[512,512]{1,0:T(8,128)(2,1)S(1)}) custom-call(s32[10,2]{1,0:T(8,128)S(1)} %flags.1, f32[264,256]{1,0:T(8,128)S(1)} %get-tuple-element.96.mine, f32[264,256]{1,0:T(8,128)S(1)} %collective-permute-done.13.other, f32[256,256]{1,0:T(8,128)S(1)} %add.14.norm), custom_call_target="tpu_custom_call" | custom-call | flops 1024 | bytes 1024 | tf_op jit(solution)/shard_map/rotation/pallas_call | solution.py:298
  128.4 7.0 %apply_all.3 = (f32[2048,256]{1,0:T(8,128)S(1)}, f32[256,2048]{1,0:T(8,128)}, f32[256,2048]{1,0:T(8,128)S(1)}, f32[256,256]{1,0:T(8,128)S(1)}, f32[1024,256]{1,0...) custom-call(f32[1024,256]{1,0:T(8,128)S(1)} %get-tuple-element.84.refs_0_, ...), custom_call_target="tpu_custom_call" | custom-call | flops 1024 | bytes 1024 | tf_op jit(solution)/shard_map/apply_all/pallas_call | solution.py:402
  135.5 1.5 collective-permute-start.21
  137.0 15.7 %collective-permute-done.16.refs_2_ = f32[1024,256]{1,0:T(8,128)S(1)} collective-permute-done((f32[1024,256]{1,0:T(8,128)S(1)}, f32[1024,256]{1,0:T(8,128)S(1)}, u32[]{:S(2)}, u32[]{:S(2)}) %collective-permute-start.16) | collective-permute-done | bytes 1048608 | tf_op jit(solution)/shard_map/ppermute | solution.py:24
  152.7 2.2 %gram.11.mine = f32[264,256]{1,0:T(8,128)S(1)} custom-call(f32[256,2048]{1,0:T(8,128)S(1)} %get-tuple-element.101.refs_0_, f32[1024,256]{1,0:T(8,128)S(1)} %collective-permute-done.15.refs_1_, f32[1024,256]{1,0:T(8,128)S(1)} %collective-permute-done.16.refs_2_, f32[256,256]{1,0:T(8,128)S(1)} %get-tuple-element.102.refs_3_), custom_call_target="tpu_custom_call" | custom-call | flops 1024 | bytes 1024 | tf_op jit(solution)/shard_map/gram/pallas_call | solution.py:211
  155.0 0.7 collective-permute-start.22
  155.7 0.8 collective-permute-done.17.other
  156.6 4.1 %rotation.11 = (bf16[512,256]{1,0:T(8,128)(2,1)S(1)}, bf16[512,256]{1,0:T(8,128)(2,1)S(1)}) custom-call(s32[10,2]{1,0:T(8,128)S(1)} %flags.1, f32[264,256]{1,0:T(8,128)S(1)} %gram.11.mine, f32[264,256]{1,0:T(8,128)S(1)} %collective-permute-done.17.other, f32[256,256]{1,0:T(8,128)S(1)} %add.14.norm), custom_call_target="tpu_custom_call" | custom-call | flops 1024 | bytes 1024 | tf_op jit(solution)/shard_map/rotation/pallas_call | solution.py:298
  160.7 6.3 %rebuild.3 = (f32[2048,256]{1,0:T(8,128)S(1)}, f32[264,256]{1,0:T(8,128)S(1)}) custom-call(f32[2048,256]{1,0:T(8,128)S(1)} %get-tuple-element.100.refs_0_, f32[1024,256]{1,0:T(8,128)S(1)} %collective-permute-done.15.refs_1_, f32[1024,256]{1,0:T(8,128)S(1)} %collective-permute-done.16.refs_2_, bf16[512,256]{1,0:T(8,128)(2,1)S(1)} %get-tuple-element.103.refs_3_, ...), custom_call_target="tpu_custom_call" | custom-call | flops 1024 | bytes 1024 | tf_op jit(solution)/shard_map/rebuild/pallas_call | solution.py:434
  167.5 1.4 collective-permute-done.19
  169.0 4.2 %rotation.12 = (bf16[512,512]{1,0:T(8,128)(2,1)S(1)}, bf16[512,512]{1,0:T(8,128)(2,1)S(1)}, f32[136,256]{1,0:T(8,128)S(1)}) custom-call(s32[10,2]{1,0:T(8,128)S(1)} %flags.1, f32[264,256]{1,0:T(8,128)S(1)} %get-tuple-element.107.mine, f32[264,256]{1,0:T(8,128)S(1)} %collective-permute-done.18.other, f32[256,256]{1,0:T(8,128)S(1)} %add.15.norm), custom_call_target="tpu_custom_call" | custom-call | flops 1024 | bytes 1024 | tf_op jit(solution)/shard_map/rotation/pallas_call | solution.py:298
  173.1 0.7 collective-permute-start.23
  173.8 0.8 apply_one.1.refs_0_
  174.6 2.6 %collective-permute-start.20 = (f32[512,256]{1,0:T(8,128)S(1)}, f32[512,256]{1,0:T(8,128)S(1)}, u32[]{:S(2)}, u32[]{:S(2)}) collective-permute-start(f32[512,256]{1,0:T(8,128)S(1)} %apply_one.1.refs_0_), channel_id=1, source_target_pairs={{0,4},{2,6},{4,8},{6,10},{8,12},{10,14},{12,0},{14,2},{1,5},{3,7},... | collective-permute-start | bytes 1572872 | tf_op jit(solution)/shard_map/ppermute | solution.py:24
  177.2 4.5 %finish.2 = (f32[2048,512]{1,0:T(8,128)}, f32[8,128]{1,0:T(8,128)S(1)}) custom-call(s32[10,2]{1,0:T(8,128)S(1)} %flags.1, f32[1024,256]{1,0:T(8,128)S(1)} %get-tuple-element.110.refs_0_, f32[512,256]{1,0:T(8,128)S(1)} %get-tuple-element.111.refs_1_, f32[512,256]{1,0:T(8,128)S(1)} %get-tuple-element.99.stay.refs_2_, ...), custom_call_target="tpu_custom_call" | custom-call | flops 1024 | bytes 1024 | tf_op jit(solution)/shard_map/finish/pallas_call | solution.py:550
  181.7 4.9 %collective-permute-done.22.refs_3_.refs_1_ = f32[512,256]{1,0:T(8,128)S(1)} collective-permute-done((f32[512,256]{1,0:T(8,128)S(1)}, f32[512,256]{1,0:T(8,128)S(1)}, u32[]{:S(2)}, u32[]{:S(2)}) %collective-permute-start.22) | collective-permute-done | bytes 524320 | tf_op jit(solution)/shard_map/ppermute | solution.py:24
  186.6 3.0 %collective-permute-done.23.message = f32[136,256]{1,0:T(8,128)S(1)} collective-permute-done((f32[136,256]{1,0:T(8,128)S(1)}, f32[136,256]{1,0:T(8,128)S(1)}, u32[]{:S(2)}, u32[]{:S(2)}) %collective-permute-start.23) | collective-permute-done | bytes 139296 | tf_op jit(solution)/shard_map/ppermute | solution.py:24
  189.7 1.3 collective-permute-done.24.other
  191.0 4.1 %rotation.13 = (bf16[512,256]{1,0:T(8,128)(2,1)S(1)}, bf16[512,256]{1,0:T(8,128)(2,1)S(1)}) custom-call(s32[10,2]{1,0:T(8,128)S(1)} %flags.1, f32[136,256]{1,0:T(8,128)S(1)} %relay.1.mine, f32[136,256]{1,0:T(8,128)S(1)} %collective-permute-done.24.other, f32[256,256]{1,0:T(8,128)S(1)} %add.15.norm), custom_call_target="tpu_custom_call" | custom-call | flops 4000000000 | bytes 1024 | tf_op jit(solution)/shard_map/rotation/pallas_call | solution.py:298
  195.2 4.3 %finish.3 = (f32[2048,512]{1,0:T(8,128)}, f32[8,128]{1,0:T(8,128)}) custom-call(s32[10,2]{1,0:T(8,128)S(1)} %flags.1, f32[1024,256]{1,0:T(8,128)S(1)} %collective-permute-done.21.refs_2_.refs_0_, f32[512,256]{1,0:T(8,128)S(1)} %collective-permute-done.22.refs_3_.refs_1_, ...), custom_call_target="tpu_custom_call", output_to_operand_aliasing={{0}: (6, {})} | custom-call | flops 1024 | bytes 1024 | tf_op jit(solution)/shard_map/finish/pallas_call | solution.py:550
  199.9 1.5 put.1
  (37 shorter events, 5.8 us)
Async XLA Ops:
  0.0 4.6 %copy-start = (s32[4,16]{1,0:T(4,128)S(1)}, s32[4,16]{1,0:T(4,128)}, u32[]{:S(2)}) copy-start(s32[4,16]{1,0:T(4,128)} %plan.1) | copy-start | bytes 772
  3.9 2.1 %collective-permute-start = (f32[264,256]{1,0:T(8,128)S(1)}, f32[264,256]{1,0:T(8,128)S(1)}, u32[]{:S(2)}, u32[]{:S(2)}) collective-permute-start(f32[264,256]{1,0:T(8,128)S(1)} %get-tuple-element.62.mine), channel_id=1, source_target_pairs={{0,1},{1,0},{2,3},{3,2},{4,5},{5,4},{6,7},{7,6},{8,9},{9,8},{10,11... | collective-permute-start | bytes 811016 | tf_op jit(solution)/shard_map/ppermute | solution.py:24
  4.4 1.6 collective-permute-start.1
  10.9 17.7 %collective-permute-start.2 = (f32[512,256]{1,0:T(8,128)S(1)}, f32[512,256]{1,0:T(8,128)S(1)}, u32[]{:S(2)}, u32[]{:S(2)}) collective-permute-start(f32[512,256]{1,0:T(8,128)S(1)} %get-tuple-element.73), channel_id=1, source_target_pairs={{0,12},{2,14},{4,0},{6,2},{8,4},{10,6},{12,8},{14,10},{1,13},{3,15... | collective-permute-start | bytes 1572872 | tf_op jit(solution)/shard_map/ppermute | solution.py:24
  18.9 20.7 %collective-permute-start.3 = (f32[512,256]{1,0:T(8,128)S(1)}, f32[512,256]{1,0:T(8,128)S(1)}, u32[]{:S(2)}, u32[]{:S(2)}) collective-permute-start(f32[512,256]{1,0:T(8,128)S(1)} %get-tuple-element.74.refs_1_), channel_id=1, source_target_pairs={{0,12},{2,14},{4,0},{6,2},{8,4},{10,6},{12,8},{14,10},{1,13},{3,15... | collective-permute-start | bytes 1572872 | tf_op jit(solution)/shard_map/ppermute | solution.py:24
  22.2 28.6 %collective-permute-start.4 = (f32[512,256]{1,0:T(8,128)S(1)}, f32[512,256]{1,0:T(8,128)S(1)}, u32[]{:S(2)}, u32[]{:S(2)}) collective-permute-start(f32[512,256]{1,0:T(8,128)S(1)} %get-tuple-element.75.refs_2_), channel_id=1, source_target_pairs={{0,12},{2,14},{4,0},{6,2},{8,4},{10,6},{12,8},{14,10},{1,13},{3,15... | collective-permute-start | bytes 1572872 | tf_op jit(solution)/shard_map/ppermute | solution.py:24
  25.6 36.5 %collective-permute-start.5 = (f32[512,256]{1,0:T(8,128)S(1)}, f32[512,256]{1,0:T(8,128)S(1)}, u32[]{:S(2)}, u32[]{:S(2)}) collective-permute-start(f32[512,256]{1,0:T(8,128)S(1)} %get-tuple-element.76.refs_3_), channel_id=1, source_target_pairs={{0,12},{2,14},{4,0},{6,2},{8,4},{10,6},{12,8},{14,10},{1,13},{3,15... | collective-permute-start | bytes 1572872 | tf_op jit(solution)/shard_map/ppermute | solution.py:24
  28.5 35.9 %collective-permute-start.7 = (f32[256,256]{1,0:T(8,128)S(1)}, f32[256,256]{1,0:T(8,128)S(1)}, u32[]{:S(2)}, u32[]{:S(2)}) collective-permute-start(f32[256,256]{1,0:T(8,128)S(1)} %get-tuple-element.81), channel_id=1, source_target_pairs={{0,1},{1,0},{2,3},{3,2},{4,5},{5,4},{6,7},{7,6},{8,9},{9,8},{10,11... | collective-permute-start | bytes 786440 | tf_op jit(solution)/shard_map/ppermute | solution.py:24
  28.6 51.7 %collective-permute-start.8 = (f32[512,256]{1,0:T(8,128)S(1)}, f32[512,256]{1,0:T(8,128)S(1)}, u32[]{:S(2)}, u32[]{:S(2)}) collective-permute-start(f32[512,256]{1,0:T(8,128)S(1)} %get-tuple-element.69.refs_0_), channel_id=1, source_target_pairs={{0,4},{2,6},{4,8},{6,10},{8,12},{10,14},{12,0},{14,2},{1,5},{3,7},... | collective-permute-start | bytes 1572872 | tf_op jit(solution)/shard_map/ppermute | solution.py:24
  39.6 46.0 %collective-permute-start.11 = (f32[512,256]{1,0:T(8,128)S(1)}, f32[512,256]{1,0:T(8,128)S(1)}, u32[]{:S(2)}, u32[]{:S(2)}) collective-permute-start(f32[512,256]{1,0:T(8,128)S(1)} %get-tuple-element.72.refs_3_), channel_id=1, source_target_pairs={{0,4},{2,6},{4,8},{6,10},{8,12},{10,14},{12,0},{14,2},{1,5},{3,7},... | collective-permute-start | bytes 1572872 | tf_op jit(solution)/shard_map/ppermute | solution.py:24
  50.8 46.0 %collective-permute-start.10 = (f32[512,256]{1,0:T(8,128)S(1)}, f32[512,256]{1,0:T(8,128)S(1)}, u32[]{:S(2)}, u32[]{:S(2)}) collective-permute-start(f32[512,256]{1,0:T(8,128)S(1)} %get-tuple-element.71.refs_2_), channel_id=1, source_target_pairs={{0,4},{2,6},{4,8},{6,10},{8,12},{10,14},{12,0},{14,2},{1,5},{3,7},... | collective-permute-start | bytes 1572872 | tf_op jit(solution)/shard_map/ppermute | solution.py:24
  62.0 45.9 %collective-permute-start.9 = (f32[512,256]{1,0:T(8,128)S(1)}, f32[512,256]{1,0:T(8,128)S(1)}, u32[]{:S(2)}, u32[]{:S(2)}) collective-permute-start(f32[512,256]{1,0:T(8,128)S(1)} %get-tuple-element.70.refs_1_), channel_id=1, source_target_pairs={{0,4},{2,6},{4,8},{6,10},{8,12},{10,14},{12,0},{14,2},{1,5},{3,7},... | collective-permute-start | bytes 1572872 | tf_op jit(solution)/shard_map/ppermute | solution.py:24
  64.4 1.6 collective-permute-start.6
  76.0 61.0 %collective-permute-start.15 = (f32[1024,256]{1,0:T(8,128)S(1)}, f32[1024,256]{1,0:T(8,128)S(1)}, u32[]{:S(2)}, u32[]{:S(2)}) collective-permute-start(f32[1024,256]{1,0:T(8,128)S(1)} %get-tuple-element.84.refs_0_), channel_id=1, source_target_pairs={{0,12},{2,14},{4,0},{6,2},{8,4},{10,6},{12,8},{14,10},{1,13},{3,15... | collective-permute-start | bytes 3145736 | tf_op jit(solution)/shard_map/ppermute | solution.py:24
  80.3 72.4 %collective-permute-start.16 = (f32[1024,256]{1,0:T(8,128)S(1)}, f32[1024,256]{1,0:T(8,128)S(1)}, u32[]{:S(2)}, u32[]{:S(2)}) collective-permute-start(f32[1024,256]{1,0:T(8,128)S(1)} %get-tuple-element.85.refs_1_), channel_id=1, source_target_pairs={{0,12},{2,14},{4,0},{6,2},{8,4},{10,6},{12,8},{14,10},{1,13},{3,15... | collective-permute-start | bytes 3145736 | tf_op jit(solution)/shard_map/ppermute | solution.py:24
  110.2 1.6 collective-permute-start.12
  122.2 2.0 %collective-permute-start.13 = (f32[264,256]{1,0:T(8,128)S(1)}, f32[264,256]{1,0:T(8,128)S(1)}, u32[]{:S(2)}, u32[]{:S(2)}) collective-permute-start(f32[264,256]{1,0:T(8,128)S(1)} %get-tuple-element.96.mine), channel_id=1, source_target_pairs={{0,1},{1,0},{2,3},{3,2},{4,5},{5,4},{6,7},{7,6},{8,9},{9,8},{10,11... | collective-permute-start | bytes 811016 | tf_op jit(solution)/shard_map/ppermute | solution.py:24
  122.4 1.8 collective-permute-start.14
  135.5 51.1 %collective-permute-start.21 = (f32[1024,256]{1,0:T(8,128)S(1)}, f32[1024,256]{1,0:T(8,128)S(1)}, u32[]{:S(2)}, u32[]{:S(2)}) collective-permute-start(f32[1024,256]{1,0:T(8,128)S(1)} %get-tuple-element.110.refs_0_), channel_id=1, source_target_pairs={{0,4},{2,6},{4,8},{6,10},{8,12},{10,14},{12,0},{14,2},{1,5},{3,7},... | collective-permute-start | bytes 3145736 | tf_op jit(solution)/shard_map/ppermute | solution.py:24
  155.0 1.6 collective-permute-start.17
  155.0 31.6 %collective-permute-start.22 = (f32[512,256]{1,0:T(8,128)S(1)}, f32[512,256]{1,0:T(8,128)S(1)}, u32[]{:S(2)}, u32[]{:S(2)}) collective-permute-start(f32[512,256]{1,0:T(8,128)S(1)} %get-tuple-element.111.refs_1_), channel_id=1, source_target_pairs={{0,4},{2,6},{4,8},{6,10},{8,12},{10,14},{12,0},{14,2},{1,5},{3,7},... | collective-permute-start | bytes 1572872 | tf_op jit(solution)/shard_map/ppermute | solution.py:24
  166.9 2.0 %collective-permute-start.18 = (f32[264,256]{1,0:T(8,128)S(1)}, f32[264,256]{1,0:T(8,128)S(1)}, u32[]{:S(2)}, u32[]{:S(2)}) collective-permute-start(f32[264,256]{1,0:T(8,128)S(1)} %get-tuple-element.107.mine), channel_id=1, source_target_pairs={{0,1},{1,0},{2,3},{3,2},{4,5},{5,4},{6,7},{7,6},{8,9},{9,8},{10,11... | collective-permute-start | bytes 811016 | tf_op jit(solution)/shard_map/ppermute | solution.py:24
  167.1 1.8 collective-permute-start.19
  173.1 16.4 %collective-permute-start.23 = (f32[136,256]{1,0:T(8,128)S(1)}, f32[136,256]{1,0:T(8,128)S(1)}, u32[]{:S(2)}, u32[]{:S(2)}) collective-permute-start(f32[136,256]{1,0:T(8,128)S(1)} %get-tuple-element.113), channel_id=1, source_target_pairs={{0,4},{2,6},{4,8},{6,10},{8,12},{10,14},{12,0},{14,2},{1,5},{3,7},... | collective-permute-start | bytes 417800 | tf_op jit(solution)/shard_map/ppermute | solution.py:24
  174.6 25.4 %collective-permute-start.20 = (f32[512,256]{1,0:T(8,128)S(1)}, f32[512,256]{1,0:T(8,128)S(1)}, u32[]{:S(2)}, u32[]{:S(2)}) collective-permute-start(f32[512,256]{1,0:T(8,128)S(1)} %apply_one.1.refs_0_), channel_id=1, source_target_pairs={{0,4},{2,6},{4,8},{6,10},{8,12},{10,14},{12,0},{14,2},{1,5},{3,7},... | collective-permute-start | bytes 1572872 | tf_op jit(solution)/shard_map/ppermute | solution.py:24
  189.6 1.4 collective-permute-start.24
where the time goes:
time: 202 us
  Pallas kernels  89.6 us (44%)
  waiting for transfers between devices  88.3 us (44%)
  starting transfers between devices  23 us (11%)
    ppermute x25, waiting for transfers between devices, shift(): lax.ppermute(value, axis, [(i, (i + by) % size) for i in range(size)])  88.3 us
    pallas_call x7, Pallas kernels, rotation(): pl.pallas_call(functools.partial(rotation_kernel, step, side, both, note,...  29.6 us
    ppermute x25, starting transfers between devices, shift(): lax.ppermute(value, axis, [(i, (i + by) % size) for i in range(size)])  23 us
    pallas_call x2, Pallas kernels, apply_all(): pl.pallas_call(functools.partial(apply_all_kernel, (len(stay), len(move))...  12.8 us
    pallas_call x2, Pallas kernels, rebuild(): pl.pallas_call(functools.partial(rebuild_kernel, (len(sent), len(raw))),...  12.6 us
    pallas_call x4, Pallas kernels, apply_both(): pl.pallas_call(functools.partial(apply_both_kernel, first), grid=(blocks,...  11.4 us
    pallas_call x2, Pallas kernels, finish(): pl.pallas_call(functools.partial(finish_kernel, (len(stay), len(move)), k...  8.79 us
    pallas_call x6, Pallas kernels, gram(): pl.pallas_call(functools.partial(gram_kernel, (len(turned), len(came), le...  6.78 us
  transfers between devices with their start and end apart: 25, of which 16 were waited for; matrix products, arithmetic and copies ran while one was open for 0% of the time, Pallas kernels for 39%

commit v1 on v0

--- a/solution.py
+++ b/solution.py
@@ -78,29 +78,37 @@
     own, stay_first = route(count, plan, device[0])
     above, _ = route(count, plan, lax.rem(device[0] + 2, count))
     below, _ = route(count, plan, lax.rem(device[0] + count - 2 % count, count))
-    for step in range(rounds):
-        flags[step, 0], flags[step, 1] = own[step]
-        sender = below[step] if step % 2 else above[step]
-        flags[rounds + step, 0] = 1 - sender[0]
-        flags[rounds + step, 1] = 1 - sender[1]
-    flags[2 * rounds, 0] = 1 - stay_first
-    flags[2 * rounds, 1] = stay_first
-    flags[2 * rounds + 1, 0] = device[1]
-    flags[2 * rounds + 1, 1] = device[1]
-
-
-def make_flags(plan, device, count):
+    senders = [(below if step % 2 else above)[step] for step in range(rounds)]
+    pairs = own + [(1 - first, 1 - send) for first, send in senders]
+    pairs += [(1 - stay_first, stay_first), (device[1], device[1])]
+    for index, pair in enumerate(pairs):
+        for half in range(2):
+            row = jnp.broadcast_to(pair[half], (1, flags.shape[1])).astype(jnp.float32)
+            flags[2 * index + half : 2 * index + half + 1, :] = row
+
+
+def make_flags(plan, device, count, width):
     return pl.pallas_call(
         functools.partial(flags_kernel, count),
         in_specs=[SMEM, SMEM],
-        out_specs=SMEM,
-        out_shape=jax.ShapeDtypeStruct((2 * plan.shape[0] + 2, 2), jnp.int32),
+        out_specs=pl.BlockSpec(memory_space=pltpu.VMEM),
+        out_shape=jax.ShapeDtypeStruct((4 * plan.shape[0] + 4, width), jnp.float32),
         compiler_params=PARAMS,
         cost_estimate=COST,
         name="flags",
     )(plan, device)
 
 
+def flag(flags, index):
+    index = index % flags.shape[0]
+    return flags[index : index + 1, :] == 1.0
+
+
+def output_half(flags, kept):
+    row = flags.shape[0] - (4 if kept else 3)
+    return jnp.max(flags[row : row + 1, :]).astype(jnp.int32)
+
+
 def column(row):
     return jnp.broadcast_to(row, (SIDE, row.shape[1])).T
 
@@ -109,7 +117,7 @@
     return jnp.sum((value * value).reshape(-1, 8, value.shape[1]), axis=0)
 
 
-def first_gram_kernel(snapshots, total, norm, held, done):
+def first_gram_kernel(snapshots, total, held, done):
     rows, columns = snapshots.shape
     width = columns // 2
 
@@ -127,8 +135,7 @@
         add_gram(total, kept.T, held[index, :, width:])
         return squares + row_sums(kept)
 
-    squares = lax.fori_loop(0, rows // BLOCK, step, jnp.zeros((8, width), jnp.float32))
-    norm[...] = column(jnp.sum(squares, axis=0, keepdims=True))
+    total[width + 8 :, :] = lax.fori_loop(0, rows // BLOCK, step, jnp.zeros((8, width), jnp.float32))
 
 
 def first_gram(snapshots):
@@ -139,11 +146,8 @@
     return pl.pallas_call(
         first_gram_kernel,
         in_specs=[pl.BlockSpec(memory_space=pl.ANY)],
-        out_specs=[vmem, vmem],
-        out_shape=[
-            jax.ShapeDtypeStruct((width + 8, width), jnp.float32),
-            jax.ShapeDtypeStruct((width, SIDE), jnp.float32),
-        ],
+        out_specs=vmem,
+        out_shape=jax.ShapeDtypeStruct((width + 16, width), jnp.float32),
         scratch_shapes=[pltpu.VMEM((blocks, BLOCK, columns), jnp.float32), pltpu.SemaphoreType.DMA((blocks,))],
         compiler_params=pltpu.CompilerParams(vmem_limit_bytes=52 * 1024 * 1024),
         cost_estimate=COST,
@@ -154,7 +158,7 @@
 def add_gram(total, turned, value):
     width = value.shape[1]
     total[:width, :] += dot3(split(turned), split(value))
-    total[width:, :] += row_sums(value)
+    total[width : width + 8, :] += row_sums(value)
 
 
 def over_blocks(lists, body, carry=None, skip=None):
@@ -219,34 +223,41 @@
     )(*args, *after)
 
 
-def rotation_kernel(step, side, both, note, piece, flags, mine, other, norm, *refs):
+def rotation_kernel(step, side, both, note, piece, flags, mine, other, *refs):
     width = mine.shape[1]
     *refs, base, inverse = refs
+    if step:
+        norm, *refs = refs
     if piece:
         snapshots, *refs, held, done = refs
         copy = pltpu.make_async_copy(snapshots.at[pl.ds(0, held.shape[0])], held, done)
         copy.start()
-    first_core = flags[flags.shape[0] - 1, 0] == 0
+    second_core = flag(flags, -1)
     if note == "read":
         one, two = mine[: width // 2, :], other[: width // 2, :]
-        total = jnp.concatenate((jnp.where(first_core, one, two), jnp.where(first_core, two, one)), axis=0)
+        total = jnp.concatenate((jnp.where(second_core, two, one), jnp.where(second_core, one, two)), axis=0)
         norm_move = mine[width // 2 : width // 2 + 1, :]
         norm_stay = column(mine[width // 2 + 1 : width // 2 + 2, :])[:, :1]
     else:
         total = mine[...] + other[...]
-        norm_move = jnp.sum(total[width:, :], axis=0, keepdims=True)
-        norm_stay = norm[:, side : side + 1]
+        norm_move = jnp.sum(total[width : width + 8, :], axis=0, keepdims=True)
+        if step:
+            norm_stay = norm[:, side : side + 1]
+        else:
+            norm_stay = column(jnp.sum(total[width + 8 :, :], axis=0, keepdims=True))[:, :1]
         total = total[:width, :]
     if note == "write":
         *refs, message = refs
-        message[: width // 2, :] = jnp.where(first_core, total[: width // 2, :], total[width // 2 :, :])
+        message[: width // 2, :] = jnp.where(second_core, total[width // 2 :, :], total[: width // 2, :])
         stay_row = norm[:, side : side + SIDE].T[:1, :]
         index = lax.broadcasted_iota(jnp.int32, (8, width), 0)
         message[width // 2 :, :] = jnp.where(index == 0, norm_move, stay_row)
     coupled = total / (norm_stay + norm_move + EPSILON)
     turned = coupled.T
-    stay_first = flags[step, 0] == (0 if note == "read" else 1)
-    send_is_stay = flags[step, 1] == (0 if note == "read" else 1)
+    stay_first = flag(flags, 2 * step)
+    send_is_stay = flag(flags, 2 * step + 1)
+    if note == "read":
+        stay_first, send_is_stay = ~stay_first, ~send_is_stay
     coupling = jnp.where(stay_first, coupled, turned)
     coupling_turned = jnp.where(stay_first, turned, coupled)
     identity = eye(width)
@@ -298,7 +309,7 @@
     return pl.pallas_call(
         functools.partial(rotation_kernel, step, side, both, note, bool(snapshots)),
         grid=(1,),
-        in_specs=[SMEM, whole(total.shape), whole(other.shape), whole(norm.shape)]
+        in_specs=[whole(value.shape) for value in (flags, total, other, *norm)]
         + [pl.BlockSpec(memory_space=pl.ANY)] * len(snapshots),
         out_specs=[whole(matrix)] * 2 + [whole(shape) for shape in shapes],
         out_shape=[jax.ShapeDtypeStruct(matrix, jnp.bfloat16)] * 2
@@ -308,7 +319,7 @@
         compiler_params=FIRST if snapshots else PARAMS,
         cost_estimate=LONG if note == "read" else COST,
         name="rotation",
-    )(flags, total, other, norm, *snapshots)
+    )(flags, total, other, *norm, *snapshots)
 
 
 def apply_both_kernel(first, joined, high, low, *refs):
@@ -453,8 +464,7 @@
     width = held.shape[1]
     token[...] = jnp.zeros_like(token)
     half = pl.ds(width, width) if kept else pl.ds(0, width)
-    column_of = flags[flags.shape[0] - 2, 1 - kept]
-    columns = pl.ds(pl.multiple_of(column_of * width, width), width)
+    columns = pl.ds(pl.multiple_of(output_half(flags, kept) * width, width), width)
 
     def write(index):
         rows = pl.ds(pl.multiple_of(index * BLOCK, BLOCK), BLOCK)
@@ -473,7 +483,7 @@
 
 def put_kernel(start, flags, came, before, out, done):
     width = came.shape[1]
-    columns = pl.ds(pl.multiple_of(flags[flags.shape[0] - 2, 1] * width, width), width)
+    columns = pl.ds(pl.multiple_of(output_half(flags, False) * width, width), width)
     copies = []
     for index in range(came.shape[0] // PUT):
         rows = pl.ds(index * PUT, PUT)
@@ -489,7 +499,7 @@
     anywhere = pl.BlockSpec(memory_space=pl.ANY)
     return pl.pallas_call(
         functools.partial(put_kernel, start),
-        in_specs=[SMEM, vmem, anywhere],
+        in_specs=[vmem, vmem, anywhere],
         out_specs=anywhere,
         out_shape=jax.ShapeDtypeStruct(before.shape, jnp.float32),
         input_output_aliases={2: 0},
@@ -549,7 +559,7 @@
     blocks = shape[0] // BLOCK
     return pl.pallas_call(
         functools.partial(finish_kernel, (len(stay), len(move)), kept, len(before) + len(after)),
-        in_specs=[SMEM] + [vmem] * (len(args) - 1) + [anywhere] * (len(before) + len(after)),
+        in_specs=[vmem] * len(args) + [anywhere] * (len(before) + len(after)),
         out_specs=[anywhere, vmem],
         out_shape=[jax.ShapeDtypeStruct(shape, jnp.float32), jax.ShapeDtypeStruct((8, SIDE), jnp.float32)],
         input_output_aliases={len(args): 0} if before else {},
@@ -566,10 +576,9 @@
     size = rows // BLOCK // PIECES
     device = lax.axis_index("pair")
     count = lax.axis_size("pair")
-    total, norm = first_gram(snapshots)
-    flags = make_flags(plan, jnp.stack((device, lax.axis_index("row"))), count)
-    norm = norm + shift(norm, "row", 1)
-    high, low, outgoing = rotation(0, 0, True, flags, total, norm, None, (snapshots,), size * BLOCK)
+    total = first_gram(snapshots)
+    flags = make_flags(plan, jnp.stack((device, lax.axis_index("row"))), count, snapshots.shape[1] // 2)
+    high, low, outgoing = rotation(0, 0, True, flags, total, (), None, (snapshots,), size * BLOCK)
     move = [shift(outgoing, "pair", -2)]
     norm = None
     held = [None] * PIECES
@@ -589,21 +598,21 @@
         norm = norm + shift(norm, "row", 1)
         if last:
             break
-        high, low = rotation(step, 0, True, flags, total, norm)
+        high, low = rotation(step, 0, True, flags, total, (norm,))
         sizes = [rows // 2, rows // 4, rows // 4] if step == rounds - 2 else [rows // 2] * 2
         new_sent, new_sent_turned, stay, stay_turned, own_norm = apply_all(stay, move, high, low, sizes)
         total = gram(sent_turned, raw, (), (own_norm,))
-        high, low = rotation(rounds + step, SIDE, False, flags, total, norm)
+        high, low = rotation(rounds + step, SIDE, False, flags, total, (norm,))
         came, total = rebuild(sent, raw, high, low, stay_turned)
         move, norm = (came,), own_norm
         sent, sent_turned = (new_sent,), (new_sent_turned,)
-    high, low, message = rotation(step, 0, True, flags, total, norm, note="write")
+    high, low, message = rotation(step, 0, True, flags, total, (norm,), note="write")
     message = shift(message, "pair", direction)
     outgoing = apply_one(stay[-1], came, high, low, (rows - stay[-1].shape[0]) // BLOCK)
     last_piece = shift(outgoing, "pair", direction)
     field, token = finish(1, flags, stay, move, high, low, (), snapshots.shape)
     message = relay(message, (outgoing, token, *raw))
-    high, low = rotation(rounds + step, SIDE, False, flags, message, norm, note="read")
+    high, low = rotation(rounds + step, SIDE, False, flags, message, (norm,), note="read")
     field, _ = finish(0, flags, raw, sent, high, low, (field,), snapshots.shape)
     return put(flags, last_piece, field, rows - last_piece.shape[0])
 

time: 202 us -> 200 us (0.990)
  Pallas kernels: 89.6 us -> 82.7 us
  waiting for transfers between devices: 88.3 us -> 93.7 us
    ppermute x25 -> x24, waiting for transfers between devices: 88.3 us -> 93.7 us  [shift(): lax.ppermute(value, axis, [(i, (i + by) % size) for i in range(size)])]
    pallas_call x7, Pallas kernels: 29.6 us -> 25.1 us  [rotation(): pl.pallas_call(functools.partial(rotation_kernel, step, side, both, note,...]
    ppermute x25 -> x24, starting transfers between devices: 23 us -> 22.9 us  [shift(): lax.ppermute(value, axis, [(i, (i + by) % size) for i in range(size)])]
  transfers between devices with their start and end apart: 25 -> 24, of which waited for: 16 -> 17; matrix products, arithmetic and copies ran while one was open for 0% -> 0% of each run, Pallas kernels for 39% -> 37%
where the time goes in v1:
time: 200 us
  waiting for transfers between devices  93.7 us (47%)
  Pallas kernels  82.7 us (41%)
  starting transfers between devices  22.9 us (11%)
    ppermute x24, waiting for transfers between devices, shift(): lax.ppermute(value, axis, [(i, (i + by) % size) for i in range(size)])  93.7 us
    pallas_call x7, Pallas kernels, rotation(): pl.pallas_call(functools.partial(rotation_kernel, step, side, both, note,...  25.1 us
    ppermute x24, starting transfers between devices, shift(): lax.ppermute(value, axis, [(i, (i + by) % size) for i in range(size)])  22.9 us
    pallas_call x2, Pallas kernels, apply_all(): pl.pallas_call(functools.partial(apply_all_kernel, (len(stay), len(move))...  12.8 us
    pallas_call x2, Pallas kernels, rebuild(): pl.pallas_call(functools.partial(rebuild_kernel, (len(sent), len(raw))),...  12.5 us
    pallas_call x4, Pallas kernels, apply_both(): pl.pallas_call(functools.partial(apply_both_kernel, first), grid=(blocks,...  11.4 us
    pallas_call x2, Pallas kernels, finish(): pl.pallas_call(functools.partial(finish_kernel, (len(stay), len(move)), k...  7.83 us
    pallas_call x6, Pallas kernels, gram(): pl.pallas_call(functools.partial(gram_kernel, (len(turned), len(came), le...  6.77 us
  transfers between devices with their start and end apart: 24, of which 17 were waited for; matrix products, arithmetic and copies ran while one was open for 0% of the time, Pallas kernels for 37%

profile of v1, /device:TPU:0, one launch (start us, length us, event | category | flops | bytes accessed | tf_op | source)
XLA Modules:
  0.0 199.9 jit_solution(4222464725563875416)
XLA Ops:
  0.0 3.8 %first_gram.1.mine = f32[272,256]{1,0:T(8,128)S(1)} custom-call(f32[2048,512]{1,0:T(8,128)} %joined.7), custom_call_target="tpu_custom_call" | custom-call | flops 1024 | bytes 1024 | tf_op jit(solution)/shard_map/first_gram/pallas_call | solution.py:146
  4.4 0.7 flags.1
  5.5 4.3 %rotation.7 = (bf16[512,512]{1,0:T(8,128)(2,1)S(1)}, bf16[512,512]{1,0:T(8,128)(2,1)S(1)}, f32[512,256]{1,0:T(8,128)S(1)}) custom-call(f32[20,256]{1,0:T(8,128)S(1)} %flags.1, f32[272,256]{1,0:T(8,128)S(1)} %first_gram.1.mine, f32[272,256]{1,0:T(8,128)S(1)} %collective-permute-done.other, f32[2048,512]{1,0:T(8,128)} %joined.7), custom_call_target="tpu_custom_call" | custom-call | flops 1024 | bytes 1024 | tf_op jit(solution)/shard_map/rotation/pallas_call | solution.py:309
  9.8 5.0 %collective-permute-start.1 = (f32[512,256]{1,0:T(8,128)S(1)}, f32[512,256]{1,0:T(8,128)S(1)}, u32[]{:S(2)}, u32[]{:S(2)}) collective-permute-start(f32[512,256]{1,0:T(8,128)S(1)} %get-tuple-element.69), channel_id=1, source_target_pairs={{0,12},{2,14},{4,0},{6,2},{8,4},{10,6},{12,8},{14,10},{1,13},{3,15... | collective-permute-start | bytes 1572872 | tf_op jit(solution)/shard_map/ppermute | solution.py:24
  14.8 2.8 %apply_both.4 = (f32[512,256]{1,0:T(8,128)S(1)}, f32[256,512]{1,0:T(8,128)S(1)}, f32[512,256]{1,0:T(8,128)S(1)}, f32[256,512]{1,0:T(8,128)S(1)}, f32[256,256]{1,0:T(8,128)S(1)}) custom-call(f32[2048,512]{1,0:T(8,128)} %joined.7, bf16[512,512]{1,0:T(8,128)(2,1)S(1)} %get-tuple-element.60.high, bf16[512,512]{1,0:T(8,128)(2,1)S(1)} %get-tuple-element.61.low), custom_call_target="tpu_custom_call" | custom-call | flops 1024 | bytes 1024 | tf_op jit(solution)/shard_map/apply_both/pallas_call | solution.py:360
  18.2 2.9 %apply_both.5 = (f32[512,256]{1,0:T(8,128)S(1)}, f32[256,512]{1,0:T(8,128)S(1)}, f32[512,256]{1,0:T(8,128)S(1)}, f32[256,512]{1,0:T(8,128)S(1)}, f32[256,256]{1,0:T(8,128)S(1)}) custom-call(f32[2048,512]{1,0:T(8,128)} %joined.7, bf16[512,512]{1,0:T(8,128)(2,1)S(1)} %get-tuple-element.60.high, bf16[512,512]{1,0:T(8,128)(2,1)S(1)} %get-tuple-element.61.low, ...), custom_call_target="tpu_custom_call" | custom-call | flops 1024 | bytes 1024 | tf_op jit(solution)/shard_map/apply_both/pallas_call | solution.py:360
  21.5 2.9 %apply_both.6 = (f32[512,256]{1,0:T(8,128)S(1)}, f32[256,512]{1,0:T(8,128)S(1)}, f32[512,256]{1,0:T(8,128)S(1)}, f32[256,512]{1,0:T(8,128)S(1)}, f32[256,256]{1,0:T(8,128)S(1)}) custom-call(f32[2048,512]{1,0:T(8,128)} %joined.7, bf16[512,512]{1,0:T(8,128)(2,1)S(1)} %get-tuple-element.60.high, bf16[512,512]{1,0:T(8,128)(2,1)S(1)} %get-tuple-element.61.low, ...), custom_call_target="tpu_custom_call" | custom-call | flops 1024 | bytes 1024 | tf_op jit(solution)/shard_map/apply_both/pallas_call | solution.py:360
  24.5 2.9 %apply_both.7 = (f32[512,256]{1,0:T(8,128)S(1)}, f32[256,512]{1,0:T(8,128)S(1)}, f32[512,256]{1,0:T(8,128)S(1)}, f32[256,512]{1,0:T(8,128)S(1)}, f32[256,256]{1,0:T(8,128)S(1)}) custom-call(f32[2048,512]{1,0:T(8,128)} %joined.7, bf16[512,512]{1,0:T(8,128)(2,1)S(1)} %get-tuple-element.60.high, bf16[512,512]{1,0:T(8,128)(2,1)S(1)} %get-tuple-element.61.low, ...), custom_call_target="tpu_custom_call" | custom-call | flops 1024 | bytes 1024 | tf_op jit(solution)/shard_map/apply_both/pallas_call | solution.py:360
  27.4 2.1 %collective-permute-start.7 = (f32[512,256]{1,0:T(8,128)S(1)}, f32[512,256]{1,0:T(8,128)S(1)}, u32[]{:S(2)}, u32[]{:S(2)}) collective-permute-start(f32[512,256]{1,0:T(8,128)S(1)} %get-tuple-element.65.refs_0_), channel_id=1, source_target_pairs={{0,4},{2,6},{4,8},{6,10},{8,12},{10,14},{12,0},{14,2},{1,5},{3,7},... | collective-permute-start | bytes 1572872 | tf_op jit(solution)/shard_map/ppermute | solution.py:24
  29.5 8.9 %collective-permute-done.2.refs_1_.refs_5_ = f32[512,256]{1,0:T(8,128)S(1)} collective-permute-done((f32[512,256]{1,0:T(8,128)S(1)}, f32[512,256]{1,0:T(8,128)S(1)}, u32[]{:S(2)}, u32[]{:S(2)}) %collective-permute-start.2) | collective-permute-done | bytes 524320 | tf_op jit(solution)/shard_map/ppermute | solution.py:24
  38.8 10.8 %collective-permute-done.3.refs_1_.refs_6_ = f32[512,256]{1,0:T(8,128)S(1)} collective-permute-done((f32[512,256]{1,0:T(8,128)S(1)}, f32[512,256]{1,0:T(8,128)S(1)}, u32[]{:S(2)}, u32[]{:S(2)}) %collective-permute-start.3) | collective-permute-done | bytes 524320 | tf_op jit(solution)/shard_map/ppermute | solution.py:24
  50.0 10.8 %collective-permute-done.4.refs_1_.refs_7_ = f32[512,256]{1,0:T(8,128)S(1)} collective-permute-done((f32[512,256]{1,0:T(8,128)S(1)}, f32[512,256]{1,0:T(8,128)S(1)}, u32[]{:S(2)}, u32[]{:S(2)}) %collective-permute-start.4) | collective-permute-done | bytes 524320 | tf_op jit(solution)/shard_map/ppermute | solution.py:24
  60.9 0.6 gram.6.refs_2_
  63.3 1.5 collective-permute-done.5.other
  64.8 3.5 %rotation.8 = (bf16[512,512]{1,0:T(8,128)(2,1)S(1)}, bf16[512,512]{1,0:T(8,128)(2,1)S(1)}) custom-call(f32[20,256]{1,0:T(8,128)S(1)} %flags.1, f32[264,256]{1,0:T(8,128)S(1)} %gram.9.mine, f32[264,256]{1,0:T(8,128)S(1)} %collective-permute-done.5.other, f32[256,256]{1,0:T(8,128)S(1)} %add.9.refs_0_), custom_call_target="tpu_custom_call" | custom-call | flops 1024 | bytes 1024 | tf_op jit(solution)/shard_map/rotation/pallas_call | solution.py:309
  68.3 5.8 %apply_all.2 = (f32[2048,256]{1,0:T(8,128)S(1)}, f32[256,2048]{1,0:T(8,128)S(1)}, f32[256,2048]{1,0:T(8,128)S(1)}, f32[256,256]{1,0:T(8,128)S(1)}, f32[1024,256]{1,0:T(8,128)S(1)}, /*index=5*/f32[1024,256]{1,0:T(8,128)S(1)}) custom-call(f32[512,256]{1,0:T(8,128)S(1)} %get-tuple-element.65.refs_0_, f32[512,256]{1,0:T(8,128)S(1)} %get-tuple-element.66.refs_1_, ...), custom_call_target="tpu_custom_call" | custom-call | flops 1024 | bytes 1024 | tf_op jit(solution)/shard_map/apply_all/pallas_call | solution.py:413
  74.1 4.3 %collective-permute-start.14 = (f32[1024,256]{1,0:T(8,128)S(1)}, f32[1024,256]{1,0:T(8,128)S(1)}, u32[]{:S(2)}, u32[]{:S(2)}) collective-permute-start(f32[1024,256]{1,0:T(8,128)S(1)} %get-tuple-element.80.refs_0_), channel_id=1, source_target_pairs={{0,12},{2,14},{4,0},{6,2},{8,4},{10,6},{12,8},{14,10},{1,13},{3,15... | collective-permute-start | bytes 3145736 | tf_op jit(solution)/shard_map/ppermute | solution.py:24
  78.5 2.0 %collective-permute-start.15 = (f32[1024,256]{1,0:T(8,128)S(1)}, f32[1024,256]{1,0:T(8,128)S(1)}, u32[]{:S(2)}, u32[]{:S(2)}) collective-permute-start(f32[1024,256]{1,0:T(8,128)S(1)} %get-tuple-element.81.refs_1_), channel_id=1, source_target_pairs={{0,12},{2,14},{4,0},{6,2},{8,4},{10,6},{12,8},{14,10},{1,13},{3,15... | collective-permute-start | bytes 3145736 | tf_op jit(solution)/shard_map/ppermute | solution.py:24
  80.5 3.9 %collective-permute-done.10.refs_7_ = f32[512,256]{1,0:T(8,128)S(1)} collective-permute-done((f32[512,256]{1,0:T(8,128)S(1)}, f32[512,256]{1,0:T(8,128)S(1)}, u32[]{:S(2)}, u32[]{:S(2)}) %collective-permute-start.10) | collective-permute-done | bytes 524320 | tf_op jit(solution)/shard_map/ppermute | solution.py:24
  84.4 11.2 %collective-permute-done.9.refs_6_ = f32[512,256]{1,0:T(8,128)S(1)} collective-permute-done((f32[512,256]{1,0:T(8,128)S(1)}, f32[512,256]{1,0:T(8,128)S(1)}, u32[]{:S(2)}, u32[]{:S(2)}) %collective-permute-start.9) | collective-permute-done | bytes 524320 | tf_op jit(solution)/shard_map/ppermute | solution.py:24
  95.6 11.1 %collective-permute-done.8.refs_5_ = f32[512,256]{1,0:T(8,128)S(1)} collective-permute-done((f32[512,256]{1,0:T(8,128)S(1)}, f32[512,256]{1,0:T(8,128)S(1)}, u32[]{:S(2)}, u32[]{:S(2)}) %collective-permute-start.8) | collective-permute-done | bytes 524320 | tf_op jit(solution)/shard_map/ppermute | solution.py:24
  106.8 2.2 %gram.10.mine = f32[264,256]{1,0:T(8,128)S(1)} custom-call(f32[256,512]{1,0:T(8,128)S(1)} %get-tuple-element.83.refs_0_, f32[256,512]{1,0:T(8,128)S(1)} %get-tuple-element.84.refs_1_, f32[256,512]{1,0:T(8,128)S(1)} %get-tuple-element.85.refs_2_, f32[256,512]{1,0:T(8,128)S(1)} %get-tuple-element.86.refs_3_, f32[512,256]{1,0:T(8,128)S(1)} %collective-permute-done.7.refs_4_, ...), custom_call_target="tpu_custom_call" | custom-call | flops 1024 | bytes 1024 | tf_op jit(solution)/shard_map/gram/pallas_call | solution.py:215
  109.1 1.5 collective-permute-done.11.other
  110.6 3.4 %rotation.9 = (bf16[512,256]{1,0:T(8,128)(2,1)S(1)}, bf16[512,256]{1,0:T(8,128)(2,1)S(1)}) custom-call(f32[20,256]{1,0:T(8,128)S(1)} %flags.1, f32[264,256]{1,0:T(8,128)S(1)} %gram.10.mine, f32[264,256]{1,0:T(8,128)S(1)} %collective-permute-done.11.other, f32[256,256]{1,0:T(8,128)S(1)} %add.9.refs_0_), custom_call_target="tpu_custom_call" | custom-call | flops 1024 | bytes 1024 | tf_op jit(solution)/shard_map/rotation/pallas_call | solution.py:309
  114.0 6.3 %rebuild.2 = (f32[2048,256]{1,0:T(8,128)S(1)}, f32[264,256]{1,0:T(8,128)S(1)}) custom-call(f32[512,256]{1,0:T(8,128)S(1)} %get-tuple-element.82.refs_0_, f32[512,256]{1,0:T(8,128)S(1)} %get-tuple-element.70.refs_1_, f32[512,256]{1,0:T(8,128)S(1)} %get-tuple-element.71.refs_2_, f32[512,256]{1,0:T(8,128)S(1)} %get-tuple-element.72.refs_3_, ...), custom_call_target="tpu_custom_call" | custom-call | flops 1024 | bytes 1024 | tf_op jit(solution)/shard_map/rebuild/pallas_call | solution.py:445
  120.9 1.4 collective-permute-done.13
  122.4 3.5 %rotation.10 = (bf16[512,512]{1,0:T(8,128)(2,1)S(1)}, bf16[512,512]{1,0:T(8,128)(2,1)S(1)}) custom-call(f32[20,256]{1,0:T(8,128)S(1)} %flags.1, f32[264,256]{1,0:T(8,128)S(1)} %get-tuple-element.92.mine, f32[264,256]{1,0:T(8,128)S(1)} %collective-permute-done.12.other, f32[256,256]{1,0:T(8,128)S(1)} %add.10.refs_0_), custom_call_target="tpu_custom_call" | custom-call | flops 1024 | bytes 1024 | tf_op jit(solution)/shard_map/rotation/pallas_call | solution.py:309
  125.9 7.0 %apply_all.3 = (f32[2048,256]{1,0:T(8,128)S(1)}, f32[256,2048]{1,0:T(8,128)}, f32[256,2048]{1,0:T(8,128)S(1)}, f32[256,256]{1,0:T(8,128)S(1)}, f32[1024,256]{1,0...) custom-call(f32[1024,256]{1,0:T(8,128)S(1)} %get-tuple-element.80.refs_0_, ...), custom_call_target="tpu_custom_call" | custom-call | flops 1024 | bytes 1024 | tf_op jit(solution)/shard_map/apply_all/pallas_call | solution.py:413
  132.9 1.5 collective-permute-start.20
  134.4 17.1 %collective-permute-done.15.refs_2_ = f32[1024,256]{1,0:T(8,128)S(1)} collective-permute-done((f32[1024,256]{1,0:T(8,128)S(1)}, f32[1024,256]{1,0:T(8,128)S(1)}, u32[]{:S(2)}, u32[]{:S(2)}) %collective-permute-start.15) | collective-permute-done | bytes 1048608 | tf_op jit(solution)/shard_map/ppermute | solution.py:24
  151.5 2.2 %gram.11.mine = f32[264,256]{1,0:T(8,128)S(1)} custom-call(f32[256,2048]{1,0:T(8,128)S(1)} %get-tuple-element.97.refs_0_, f32[1024,256]{1,0:T(8,128)S(1)} %collective-permute-done.14.refs_1_, f32[1024,256]{1,0:T(8,128)S(1)} %collective-permute-done.15.refs_2_, f32[256,256]{1,0:T(8,128)S(1)} %get-tuple-element.98.refs_3_), custom_call_target="tpu_custom_call" | custom-call | flops 1024 | bytes 1024 | tf_op jit(solution)/shard_map/gram/pallas_call | solution.py:215
  153.8 0.7 collective-permute-start.21
  154.6 0.8 collective-permute-done.16.other
  155.4 3.4 %rotation.11 = (bf16[512,256]{1,0:T(8,128)(2,1)S(1)}, bf16[512,256]{1,0:T(8,128)(2,1)S(1)}) custom-call(f32[20,256]{1,0:T(8,128)S(1)} %flags.1, f32[264,256]{1,0:T(8,128)S(1)} %gram.11.mine, f32[264,256]{1,0:T(8,128)S(1)} %collective-permute-done.16.other, f32[256,256]{1,0:T(8,128)S(1)} %add.10.refs_0_), custom_call_target="tpu_custom_call" | custom-call | flops 1024 | bytes 1024 | tf_op jit(solution)/shard_map/rotation/pallas_call | solution.py:309
  158.8 6.3 %rebuild.3 = (f32[2048,256]{1,0:T(8,128)S(1)}, f32[264,256]{1,0:T(8,128)S(1)}) custom-call(f32[2048,256]{1,0:T(8,128)S(1)} %get-tuple-element.96.refs_0_, f32[1024,256]{1,0:T(8,128)S(1)} %collective-permute-done.14.refs_1_, f32[1024,256]{1,0:T(8,128)S(1)} %collective-permute-done.15.refs_2_, bf16[512,256]{1,0:T(8,128)(2,1)S(1)} %get-tuple-element.99.refs_3_, ...), custom_call_target="tpu_custom_call" | custom-call | flops 1024 | bytes 1024 | tf_op jit(solution)/shard_map/rebuild/pallas_call | solution.py:445
  165.6 1.4 collective-permute-done.18
  167.1 3.5 %rotation.12 = (bf16[512,512]{1,0:T(8,128)(2,1)S(1)}, bf16[512,512]{1,0:T(8,128)(2,1)S(1)}, f32[136,256]{1,0:T(8,128)S(1)}) custom-call(f32[20,256]{1,0:T(8,128)S(1)} %flags.1, f32[264,256]{1,0:T(8,128)S(1)} %get-tuple-element.103.mine, f32[264,256]{1,0:T(8,128)S(1)} %collective-permute-done.17.other, f32[256,256]{1,0:T(8,128)S(1)} %add.11.refs_0_), custom_call_target="tpu_custom_call" | custom-call | flops 1024 | bytes 1024 | tf_op jit(solution)/shard_map/rotation/pallas_call | solution.py:309
  170.6 0.7 collective-permute-start.22
  171.3 0.8 apply_one.1.refs_0_
  172.1 2.6 %collective-permute-start.19 = (f32[512,256]{1,0:T(8,128)S(1)}, f32[512,256]{1,0:T(8,128)S(1)}, u32[]{:S(2)}, u32[]{:S(2)}) collective-permute-start(f32[512,256]{1,0:T(8,128)S(1)} %apply_one.1.refs_0_), channel_id=1, source_target_pairs={{0,4},{2,6},{4,8},{6,10},{8,12},{10,14},{12,0},{14,2},{1,5},{3,7},... | collective-permute-start | bytes 1572872 | tf_op jit(solution)/shard_map/ppermute | solution.py:24
  174.7 4.1 %finish.2 = (f32[2048,512]{1,0:T(8,128)}, f32[8,128]{1,0:T(8,128)S(1)}) custom-call(f32[20,256]{1,0:T(8,128)S(1)} %flags.1, f32[1024,256]{1,0:T(8,128)S(1)} %get-tuple-element.106.refs_0_, f32[512,256]{1,0:T(8,128)S(1)} %get-tuple-element.107.refs_1_, f32[512,256]{1,0:T(8,128)S(1)} %get-tuple-element.95.stay.refs_2_, ...), custom_call_target="tpu_custom_call" | custom-call | flops 1024 | bytes 1024 | tf_op jit(solution)/shard_map/finish/pallas_call | solution.py:560
  178.8 6.6 %collective-permute-done.21.refs_3_.refs_1_ = f32[512,256]{1,0:T(8,128)S(1)} collective-permute-done((f32[512,256]{1,0:T(8,128)S(1)}, f32[512,256]{1,0:T(8,128)S(1)}, u32[]{:S(2)}, u32[]{:S(2)}) %collective-permute-start.21) | collective-permute-done | bytes 524320 | tf_op jit(solution)/shard_map/ppermute | solution.py:24
  185.4 3.0 %collective-permute-done.22.message = f32[136,256]{1,0:T(8,128)S(1)} collective-permute-done((f32[136,256]{1,0:T(8,128)S(1)}, f32[136,256]{1,0:T(8,128)S(1)}, u32[]{:S(2)}, u32[]{:S(2)}) %collective-permute-start.22) | collective-permute-done | bytes 139296 | tf_op jit(solution)/shard_map/ppermute | solution.py:24
  188.5 1.3 collective-permute-done.23.other
  189.8 3.5 %rotation.13 = (bf16[512,256]{1,0:T(8,128)(2,1)S(1)}, bf16[512,256]{1,0:T(8,128)(2,1)S(1)}) custom-call(f32[20,256]{1,0:T(8,128)S(1)} %flags.1, f32[136,256]{1,0:T(8,128)S(1)} %relay.1.mine, f32[136,256]{1,0:T(8,128)S(1)} %collective-permute-done.23.other, f32[256,256]{1,0:T(8,128)S(1)} %add.11.refs_0_), custom_call_target="tpu_custom_call" | custom-call | flops 4000000000 | bytes 1024 | tf_op jit(solution)/shard_map/rotation/pallas_call | solution.py:309
  193.3 3.7 %finish.3 = (f32[2048,512]{1,0:T(8,128)}, f32[8,128]{1,0:T(8,128)}) custom-call(f32[20,256]{1,0:T(8,128)S(1)} %flags.1, f32[1024,256]{1,0:T(8,128)S(1)} %collective-permute-done.20.refs_2_.refs_0_, f32[512,256]{1,0:T(8,128)S(1)} %collective-permute-done.21.refs_3_.refs_1_, ...), custom_call_target="tpu_custom_call", output_to_operand_aliasing={{0}: (6, {})} | custom-call | flops 1024 | bytes 1024 | tf_op jit(solution)/shard_map/finish/pallas_call | solution.py:560
  197.1 1.8 collective-permute-done.19.came
  198.8 1.0 put.1
  (34 shorter events, 6.3 us)
Async XLA Ops:
  0.0 4.4 %copy-start = (s32[4,16]{1,0:T(4,128)S(1)}, s32[4,16]{1,0:T(4,128)}, u32[]{:S(2)}) copy-start(s32[4,16]{1,0:T(4,128)} %plan.1) | copy-start | bytes 772
  3.8 1.7 collective-permute-start
  9.8 17.6 %collective-permute-start.1 = (f32[512,256]{1,0:T(8,128)S(1)}, f32[512,256]{1,0:T(8,128)S(1)}, u32[]{:S(2)}, u32[]{:S(2)}) collective-permute-start(f32[512,256]{1,0:T(8,128)S(1)} %get-tuple-element.69), channel_id=1, source_target_pairs={{0,12},{2,14},{4,0},{6,2},{8,4},{10,6},{12,8},{14,10},{1,13},{3,15... | collective-permute-start | bytes 1572872 | tf_op jit(solution)/shard_map/ppermute | solution.py:24
  17.7 20.7 %collective-permute-start.2 = (f32[512,256]{1,0:T(8,128)S(1)}, f32[512,256]{1,0:T(8,128)S(1)}, u32[]{:S(2)}, u32[]{:S(2)}) collective-permute-start(f32[512,256]{1,0:T(8,128)S(1)} %get-tuple-element.70.refs_1_), channel_id=1, source_target_pairs={{0,12},{2,14},{4,0},{6,2},{8,4},{10,6},{12,8},{14,10},{1,13},{3,15... | collective-permute-start | bytes 1572872 | tf_op jit(solution)/shard_map/ppermute | solution.py:24
  21.0 28.6 %collective-permute-start.3 = (f32[512,256]{1,0:T(8,128)S(1)}, f32[512,256]{1,0:T(8,128)S(1)}, u32[]{:S(2)}, u32[]{:S(2)}) collective-permute-start(f32[512,256]{1,0:T(8,128)S(1)} %get-tuple-element.71.refs_2_), channel_id=1, source_target_pairs={{0,12},{2,14},{4,0},{6,2},{8,4},{10,6},{12,8},{14,10},{1,13},{3,15... | collective-permute-start | bytes 1572872 | tf_op jit(solution)/shard_map/ppermute | solution.py:24
  24.4 36.5 %collective-permute-start.4 = (f32[512,256]{1,0:T(8,128)S(1)}, f32[512,256]{1,0:T(8,128)S(1)}, u32[]{:S(2)}, u32[]{:S(2)}) collective-permute-start(f32[512,256]{1,0:T(8,128)S(1)} %get-tuple-element.72.refs_3_), channel_id=1, source_target_pairs={{0,12},{2,14},{4,0},{6,2},{8,4},{10,6},{12,8},{14,10},{1,13},{3,15... | collective-permute-start | bytes 1572872 | tf_op jit(solution)/shard_map/ppermute | solution.py:24
  27.3 35.9 %collective-permute-start.6 = (f32[256,256]{1,0:T(8,128)S(1)}, f32[256,256]{1,0:T(8,128)S(1)}, u32[]{:S(2)}, u32[]{:S(2)}) collective-permute-start(f32[256,256]{1,0:T(8,128)S(1)} %get-tuple-element.77), channel_id=1, source_target_pairs={{0,1},{1,0},{2,3},{3,2},{4,5},{5,4},{6,7},{7,6},{8,9},{9,8},{10,11... | collective-permute-start | bytes 786440 | tf_op jit(solution)/shard_map/ppermute | solution.py:24
  27.4 51.0 %collective-permute-start.7 = (f32[512,256]{1,0:T(8,128)S(1)}, f32[512,256]{1,0:T(8,128)S(1)}, u32[]{:S(2)}, u32[]{:S(2)}) collective-permute-start(f32[512,256]{1,0:T(8,128)S(1)} %get-tuple-element.65.refs_0_), channel_id=1, source_target_pairs={{0,4},{2,6},{4,8},{6,10},{8,12},{10,14},{12,0},{14,2},{1,5},{3,7},... | collective-permute-start | bytes 1572872 | tf_op jit(solution)/shard_map/ppermute | solution.py:24
  38.4 46.0 %collective-permute-start.10 = (f32[512,256]{1,0:T(8,128)S(1)}, f32[512,256]{1,0:T(8,128)S(1)}, u32[]{:S(2)}, u32[]{:S(2)}) collective-permute-start(f32[512,256]{1,0:T(8,128)S(1)} %get-tuple-element.68.refs_3_), channel_id=1, source_target_pairs={{0,4},{2,6},{4,8},{6,10},{8,12},{10,14},{12,0},{14,2},{1,5},{3,7},... | collective-permute-start | bytes 1572872 | tf_op jit(solution)/shard_map/ppermute | solution.py:24
  49.6 46.0 %collective-permute-start.9 = (f32[512,256]{1,0:T(8,128)S(1)}, f32[512,256]{1,0:T(8,128)S(1)}, u32[]{:S(2)}, u32[]{:S(2)}) collective-permute-start(f32[512,256]{1,0:T(8,128)S(1)} %get-tuple-element.67.refs_2_), channel_id=1, source_target_pairs={{0,4},{2,6},{4,8},{6,10},{8,12},{10,14},{12,0},{14,2},{1,5},{3,7},... | collective-permute-start | bytes 1572872 | tf_op jit(solution)/shard_map/ppermute | solution.py:24
  60.9 45.9 %collective-permute-start.8 = (f32[512,256]{1,0:T(8,128)S(1)}, f32[512,256]{1,0:T(8,128)S(1)}, u32[]{:S(2)}, u32[]{:S(2)}) collective-permute-start(f32[512,256]{1,0:T(8,128)S(1)} %get-tuple-element.66.refs_1_), channel_id=1, source_target_pairs={{0,4},{2,6},{4,8},{6,10},{8,12},{10,14},{12,0},{14,2},{1,5},{3,7},... | collective-permute-start | bytes 1572872 | tf_op jit(solution)/shard_map/ppermute | solution.py:24
  63.2 1.6 collective-permute-start.5
  74.1 60.3 %collective-permute-start.14 = (f32[1024,256]{1,0:T(8,128)S(1)}, f32[1024,256]{1,0:T(8,128)S(1)}, u32[]{:S(2)}, u32[]{:S(2)}) collective-permute-start(f32[1024,256]{1,0:T(8,128)S(1)} %get-tuple-element.80.refs_0_), channel_id=1, source_target_pairs={{0,12},{2,14},{4,0},{6,2},{8,4},{10,6},{12,8},{14,10},{1,13},{3,15... | collective-permute-start | bytes 3145736 | tf_op jit(solution)/shard_map/ppermute | solution.py:24
  78.5 73.1 %collective-permute-start.15 = (f32[1024,256]{1,0:T(8,128)S(1)}, f32[1024,256]{1,0:T(8,128)S(1)}, u32[]{:S(2)}, u32[]{:S(2)}) collective-permute-start(f32[1024,256]{1,0:T(8,128)S(1)} %get-tuple-element.81.refs_1_), channel_id=1, source_target_pairs={{0,12},{2,14},{4,0},{6,2},{8,4},{10,6},{12,8},{14,10},{1,13},{3,15... | collective-permute-start | bytes 3145736 | tf_op jit(solution)/shard_map/ppermute | solution.py:24
  109.0 1.6 collective-permute-start.11
  120.3 2.0 %collective-permute-start.12 = (f32[264,256]{1,0:T(8,128)S(1)}, f32[264,256]{1,0:T(8,128)S(1)}, u32[]{:S(2)}, u32[]{:S(2)}) collective-permute-start(f32[264,256]{1,0:T(8,128)S(1)} %get-tuple-element.92.mine), channel_id=1, source_target_pairs={{0,1},{1,0},{2,3},{3,2},{4,5},{5,4},{6,7},{7,6},{8,9},{9,8},{10,11... | collective-permute-start | bytes 811016 | tf_op jit(solution)/shard_map/ppermute | solution.py:24
  120.5 1.8 collective-permute-start.13
  132.9 52.5 %collective-permute-start.20 = (f32[1024,256]{1,0:T(8,128)S(1)}, f32[1024,256]{1,0:T(8,128)S(1)}, u32[]{:S(2)}, u32[]{:S(2)}) collective-permute-start(f32[1024,256]{1,0:T(8,128)S(1)} %get-tuple-element.106.refs_0_), channel_id=1, source_target_pairs={{0,4},{2,6},{4,8},{6,10},{8,12},{10,14},{12,0},{14,2},{1,5},{3,7},... | collective-permute-start | bytes 3145736 | tf_op jit(solution)/shard_map/ppermute | solution.py:24
  153.8 1.6 collective-permute-start.16
  153.8 31.6 %collective-permute-start.21 = (f32[512,256]{1,0:T(8,128)S(1)}, f32[512,256]{1,0:T(8,128)S(1)}, u32[]{:S(2)}, u32[]{:S(2)}) collective-permute-start(f32[512,256]{1,0:T(8,128)S(1)} %get-tuple-element.107.refs_1_), channel_id=1, source_target_pairs={{0,4},{2,6},{4,8},{6,10},{8,12},{10,14},{12,0},{14,2},{1,5},{3,7},... | collective-permute-start | bytes 1572872 | tf_op jit(solution)/shard_map/ppermute | solution.py:24
  165.1 2.0 %collective-permute-start.17 = (f32[264,256]{1,0:T(8,128)S(1)}, f32[264,256]{1,0:T(8,128)S(1)}, u32[]{:S(2)}, u32[]{:S(2)}) collective-permute-start(f32[264,256]{1,0:T(8,128)S(1)} %get-tuple-element.103.mine), channel_id=1, source_target_pairs={{0,1},{1,0},{2,3},{3,2},{4,5},{5,4},{6,7},{7,6},{8,9},{9,8},{10,11... | collective-permute-start | bytes 811016 | tf_op jit(solution)/shard_map/ppermute | solution.py:24
  165.3 1.8 collective-permute-start.18
  170.6 17.8 %collective-permute-start.22 = (f32[136,256]{1,0:T(8,128)S(1)}, f32[136,256]{1,0:T(8,128)S(1)}, u32[]{:S(2)}, u32[]{:S(2)}) collective-permute-start(f32[136,256]{1,0:T(8,128)S(1)} %get-tuple-element.109), channel_id=1, source_target_pairs={{0,4},{2,6},{4,8},{6,10},{8,12},{10,14},{12,0},{14,2},{1,5},{3,7},... | collective-permute-start | bytes 417800 | tf_op jit(solution)/shard_map/ppermute | solution.py:24
  172.1 26.7 %collective-permute-start.19 = (f32[512,256]{1,0:T(8,128)S(1)}, f32[512,256]{1,0:T(8,128)S(1)}, u32[]{:S(2)}, u32[]{:S(2)}) collective-permute-start(f32[512,256]{1,0:T(8,128)S(1)} %apply_one.1.refs_0_), channel_id=1, source_target_pairs={{0,4},{2,6},{4,8},{6,10},{8,12},{10,14},{12,0},{14,2},{1,5},{3,7},... | collective-permute-start | bytes 1572872 | tf_op jit(solution)/shard_map/ppermute | solution.py:24
  188.4 1.4 collective-permute-start.23

commit v2 on v1

--- a/solution.py
+++ b/solution.py
@@ -13,6 +13,7 @@
 PIECES = 4
 SIDE = 128
 PUT = 64
+GROUP = 4
 FIRST_MIB = 48
 PARAMS = pltpu.CompilerParams(vmem_limit_bytes=12 * 1024 * 1024)
 LARGE = pltpu.CompilerParams(vmem_limit_bytes=24 * 1024 * 1024)
@@ -123,19 +124,21 @@
 
     def read(index):
         rows = pl.ds(pl.multiple_of(index * BLOCK, BLOCK), BLOCK)
-        return pltpu.make_async_copy(snapshots.at[rows], held.at[index], done.at[index])
+        return pltpu.make_async_copy(snapshots.at[rows], held.at[rows], done.at[index])
 
     for index in range(rows // BLOCK):
         read(index).start()
     total[...] = jnp.zeros_like(total)
 
     def step(index, squares):
-        read(index).wait()
-        kept = held[index, :, :width]
-        add_gram(total, kept.T, held[index, :, width:])
+        for part in range(GROUP):
+            read(index * GROUP + part).wait()
+        here = pl.ds(pl.multiple_of(index * GROUP * BLOCK, BLOCK), GROUP * BLOCK)
+        kept = held[here, :width]
+        add_gram(total, kept.T, held[here, width:])
         return squares + row_sums(kept)
 
-    total[width + 8 :, :] = lax.fori_loop(0, rows // BLOCK, step, jnp.zeros((8, width), jnp.float32))
+    total[width + 8 :, :] = lax.fori_loop(0, rows // (GROUP * BLOCK), step, jnp.zeros((8, width), jnp.float32))
 
 
 def first_gram(snapshots):
@@ -148,7 +151,7 @@
         in_specs=[pl.BlockSpec(memory_space=pl.ANY)],
         out_specs=vmem,
         out_shape=jax.ShapeDtypeStruct((width + 16, width), jnp.float32),
-        scratch_shapes=[pltpu.VMEM((blocks, BLOCK, columns), jnp.float32), pltpu.SemaphoreType.DMA((blocks,))],
+        scratch_shapes=[pltpu.VMEM((rows, columns), jnp.float32), pltpu.SemaphoreType.DMA((blocks,))],
         compiler_params=pltpu.CompilerParams(vmem_limit_bytes=52 * 1024 * 1024),
         cost_estimate=COST,
         name="first_gram",
@@ -225,7 +228,7 @@
 
 def rotation_kernel(step, side, both, note, piece, flags, mine, other, *refs):
     width = mine.shape[1]
-    *refs, base, inverse = refs
+    *refs, base, product = refs
     if step:
         norm, *refs = refs
     if piece:
@@ -264,19 +267,19 @@
     scale = 1.0 / (1.0 + jnp.sum(coupled * coupled))
     left, right = split(coupling_turned), split(coupling)
     base[...] = scale * (identity + dot3(right, left))
-    inverse[...] = scale * identity
+    product[...] = scale * coupling_turned
 
     def sweep(_, carry):
         pair = split(base[...])
-        inverse[...] = 2.0 * inverse[...] - dot3(split(inverse[...]), pair)
+        product[...] = 2.0 * product[...] - dot3(split(product[...]), pair)
         base[...] = 2.0 * base[...] - dot3(pair, pair)
         return carry
 
     lax.fori_loop(0, NS_ITERS, sweep, 0)
-    inverse = inverse[...]
-    product_turned = dot3(left, split(inverse))
-    second_second = identity - 2.0 * dot3(split(product_turned), right)
-    first_first = 2.0 * inverse - identity
+    product_turned = product[...]
+    pair = split(product_turned)
+    second_second = identity - 2.0 * dot3(pair, right)
+    first_first = 2.0 * (base[...] - dot3(right, pair)) - identity
     first_second = 2.0 * product_turned.T
     second_first = -2.0 * product_turned
     stay_stay = jnp.where(stay_first, first_first, second_second)

time: 200 us -> 199 us (level)
  Pallas kernels: 82.7 us -> 80.5 us
  transfers between devices with their start and end apart: 24 -> 24, of which waited for: 17 -> 17; matrix products, arithmetic and copies ran while one was open for 0% -> 0% of each run, Pallas kernels for 37% -> 36%
where the time goes in v2:
time: 199 us
  waiting for transfers between devices  95 us (48%)
  Pallas kernels  80.5 us (40%)
  starting transfers between devices  22.9 us (12%)
    ppermute x24, waiting for transfers between devices, shift(): lax.ppermute(value, axis, [(i, (i + by) % size) for i in range(size)])  95 us
    pallas_call x7, Pallas kernels, rotation(): pl.pallas_call(functools.partial(rotation_kernel, step, side, both, note,...  23.6 us
    ppermute x24, starting transfers between devices, shift(): lax.ppermute(value, axis, [(i, (i + by) % size) for i in range(size)])  22.9 us
    pallas_call x2, Pallas kernels, apply_all(): pl.pallas_call(functools.partial(apply_all_kernel, (len(stay), len(move))...  12.8 us
    pallas_call x2, Pallas kernels, rebuild(): pl.pallas_call(functools.partial(rebuild_kernel, (len(sent), len(raw))),...  12.5 us
    pallas_call x4, Pallas kernels, apply_both(): pl.pallas_call(functools.partial(apply_both_kernel, first), grid=(blocks,...  11.4 us
    pallas_call x2, Pallas kernels, finish(): pl.pallas_call(functools.partial(finish_kernel, (len(stay), len(move)), k...  7.84 us
    pallas_call x6, Pallas kernels, gram(): pl.pallas_call(functools.partial(gram_kernel, (len(turned), len(came), le...  6.76 us
  transfers between devices with their start and end apart: 24, of which 17 were waited for; matrix products, arithmetic and copies ran while one was open for 0% of the time, Pallas kernels for 36%

profile of v2, /device:TPU:0, one launch (start us, length us, event | category | flops | bytes accessed | tf_op | source)
XLA Modules:
  0.0 199.0 jit_solution(10730309924267659044)
XLA Ops:
  0.0 3.1 %first_gram.1.mine = f32[272,256]{1,0:T(8,128)S(1)} custom-call(f32[2048,512]{1,0:T(8,128)} %joined.7), custom_call_target="tpu_custom_call" | custom-call | flops 1024 | bytes 1024 | tf_op jit(solution)/shard_map/first_gram/pallas_call | solution.py:149
  3.7 0.7 flags.1
  4.8 4.0 %rotation.7 = (bf16[512,512]{1,0:T(8,128)(2,1)S(1)}, bf16[512,512]{1,0:T(8,128)(2,1)S(1)}, f32[512,256]{1,0:T(8,128)S(1)}) custom-call(f32[20,256]{1,0:T(8,128)S(1)} %flags.1, f32[272,256]{1,0:T(8,128)S(1)} %first_gram.1.mine, f32[272,256]{1,0:T(8,128)S(1)} %collective-permute-done.other, f32[2048,512]{1,0:T(8,128)} %joined.7), custom_call_target="tpu_custom_call" | custom-call | flops 1024 | bytes 1024 | tf_op jit(solution)/shard_map/rotation/pallas_call | solution.py:312
  8.8 5.0 %collective-permute-start.1 = (f32[512,256]{1,0:T(8,128)S(1)}, f32[512,256]{1,0:T(8,128)S(1)}, u32[]{:S(2)}, u32[]{:S(2)}) collective-permute-start(f32[512,256]{1,0:T(8,128)S(1)} %get-tuple-element.69), channel_id=1, source_target_pairs={{0,12},{2,14},{4,0},{6,2},{8,4},{10,6},{12,8},{14,10},{1,13},{3,15... | collective-permute-start | bytes 1572872 | tf_op jit(solution)/shard_map/ppermute | solution.py:25
  13.9 2.8 %apply_both.4 = (f32[512,256]{1,0:T(8,128)S(1)}, f32[256,512]{1,0:T(8,128)S(1)}, f32[512,256]{1,0:T(8,128)S(1)}, f32[256,512]{1,0:T(8,128)S(1)}, f32[256,256]{1,0:T(8,128)S(1)}) custom-call(f32[2048,512]{1,0:T(8,128)} %joined.7, bf16[512,512]{1,0:T(8,128)(2,1)S(1)} %get-tuple-element.60.high, bf16[512,512]{1,0:T(8,128)(2,1)S(1)} %get-tuple-element.61.low), custom_call_target="tpu_custom_call" | custom-call | flops 1024 | bytes 1024 | tf_op jit(solution)/shard_map/apply_both/pallas_call | solution.py:363
  17.2 2.9 %apply_both.5 = (f32[512,256]{1,0:T(8,128)S(1)}, f32[256,512]{1,0:T(8,128)S(1)}, f32[512,256]{1,0:T(8,128)S(1)}, f32[256,512]{1,0:T(8,128)S(1)}, f32[256,256]{1,0:T(8,128)S(1)}) custom-call(f32[2048,512]{1,0:T(8,128)} %joined.7, bf16[512,512]{1,0:T(8,128)(2,1)S(1)} %get-tuple-element.60.high, bf16[512,512]{1,0:T(8,128)(2,1)S(1)} %get-tuple-element.61.low, ...), custom_call_target="tpu_custom_call" | custom-call | flops 1024 | bytes 1024 | tf_op jit(solution)/shard_map/apply_both/pallas_call | solution.py:363
  20.6 2.9 %apply_both.6 = (f32[512,256]{1,0:T(8,128)S(1)}, f32[256,512]{1,0:T(8,128)S(1)}, f32[512,256]{1,0:T(8,128)S(1)}, f32[256,512]{1,0:T(8,128)S(1)}, f32[256,256]{1,0:T(8,128)S(1)}) custom-call(f32[2048,512]{1,0:T(8,128)} %joined.7, bf16[512,512]{1,0:T(8,128)(2,1)S(1)} %get-tuple-element.60.high, bf16[512,512]{1,0:T(8,128)(2,1)S(1)} %get-tuple-element.61.low, ...), custom_call_target="tpu_custom_call" | custom-call | flops 1024 | bytes 1024 | tf_op jit(solution)/shard_map/apply_both/pallas_call | solution.py:363
  23.5 2.9 %apply_both.7 = (f32[512,256]{1,0:T(8,128)S(1)}, f32[256,512]{1,0:T(8,128)S(1)}, f32[512,256]{1,0:T(8,128)S(1)}, f32[256,512]{1,0:T(8,128)S(1)}, f32[256,256]{1,0:T(8,128)S(1)}) custom-call(f32[2048,512]{1,0:T(8,128)} %joined.7, bf16[512,512]{1,0:T(8,128)(2,1)S(1)} %get-tuple-element.60.high, bf16[512,512]{1,0:T(8,128)(2,1)S(1)} %get-tuple-element.61.low, ...), custom_call_target="tpu_custom_call" | custom-call | flops 1024 | bytes 1024 | tf_op jit(solution)/shard_map/apply_both/pallas_call | solution.py:363
  26.5 2.1 %collective-permute-start.7 = (f32[512,256]{1,0:T(8,128)S(1)}, f32[512,256]{1,0:T(8,128)S(1)}, u32[]{:S(2)}, u32[]{:S(2)}) collective-permute-start(f32[512,256]{1,0:T(8,128)S(1)} %get-tuple-element.65.refs_0_), channel_id=1, source_target_pairs={{0,4},{2,6},{4,8},{6,10},{8,12},{10,14},{12,0},{14,2},{1,5},{3,7},... | collective-permute-start | bytes 1572872 | tf_op jit(solution)/shard_map/ppermute | solution.py:25
  28.5 8.9 %collective-permute-done.2.refs_1_.refs_5_ = f32[512,256]{1,0:T(8,128)S(1)} collective-permute-done((f32[512,256]{1,0:T(8,128)S(1)}, f32[512,256]{1,0:T(8,128)S(1)}, u32[]{:S(2)}, u32[]{:S(2)}) %collective-permute-start.2) | collective-permute-done | bytes 524320 | tf_op jit(solution)/shard_map/ppermute | solution.py:25
  37.9 10.8 %collective-permute-done.3.refs_1_.refs_6_ = f32[512,256]{1,0:T(8,128)S(1)} collective-permute-done((f32[512,256]{1,0:T(8,128)S(1)}, f32[512,256]{1,0:T(8,128)S(1)}, u32[]{:S(2)}, u32[]{:S(2)}) %collective-permute-start.3) | collective-permute-done | bytes 524320 | tf_op jit(solution)/shard_map/ppermute | solution.py:25
  49.1 10.8 %collective-permute-done.4.refs_1_.refs_7_ = f32[512,256]{1,0:T(8,128)S(1)} collective-permute-done((f32[512,256]{1,0:T(8,128)S(1)}, f32[512,256]{1,0:T(8,128)S(1)}, u32[]{:S(2)}, u32[]{:S(2)}) %collective-permute-start.4) | collective-permute-done | bytes 524320 | tf_op jit(solution)/shard_map/ppermute | solution.py:25
  60.5 0.6 gram.7.refs_2_
  62.4 1.5 collective-permute-done.5.other
  63.9 3.3 %rotation.8 = (bf16[512,512]{1,0:T(8,128)(2,1)S(1)}, bf16[512,512]{1,0:T(8,128)(2,1)S(1)}) custom-call(f32[20,256]{1,0:T(8,128)S(1)} %flags.1, f32[264,256]{1,0:T(8,128)S(1)} %gram.9.mine, f32[264,256]{1,0:T(8,128)S(1)} %collective-permute-done.5.other, f32[256,256]{1,0:T(8,128)S(1)} %add.9.refs_0_), custom_call_target="tpu_custom_call" | custom-call | flops 1024 | bytes 1024 | tf_op jit(solution)/shard_map/rotation/pallas_call | solution.py:312
  67.1 5.8 %apply_all.2 = (f32[2048,256]{1,0:T(8,128)S(1)}, f32[256,2048]{1,0:T(8,128)S(1)}, f32[256,2048]{1,0:T(8,128)S(1)}, f32[256,256]{1,0:T(8,128)S(1)}, f32[1024,256]{1,0:T(8,128)S(1)}, /*index=5*/f32[1024,256]{1,0:T(8,128)S(1)}) custom-call(f32[512,256]{1,0:T(8,128)S(1)} %get-tuple-element.65.refs_0_, f32[512,256]{1,0:T(8,128)S(1)} %get-tuple-element.66.refs_1_, ...), custom_call_target="tpu_custom_call" | custom-call | flops 1024 | bytes 1024 | tf_op jit(solution)/shard_map/apply_all/pallas_call | solution.py:416
  73.0 4.3 %collective-permute-start.14 = (f32[1024,256]{1,0:T(8,128)S(1)}, f32[1024,256]{1,0:T(8,128)S(1)}, u32[]{:S(2)}, u32[]{:S(2)}) collective-permute-start(f32[1024,256]{1,0:T(8,128)S(1)} %get-tuple-element.80.refs_0_), channel_id=1, source_target_pairs={{0,12},{2,14},{4,0},{6,2},{8,4},{10,6},{12,8},{14,10},{1,13},{3,15... | collective-permute-start | bytes 3145736 | tf_op jit(solution)/shard_map/ppermute | solution.py:25
  77.3 2.0 %collective-permute-start.15 = (f32[1024,256]{1,0:T(8,128)S(1)}, f32[1024,256]{1,0:T(8,128)S(1)}, u32[]{:S(2)}, u32[]{:S(2)}) collective-permute-start(f32[1024,256]{1,0:T(8,128)S(1)} %get-tuple-element.81.refs_1_), channel_id=1, source_target_pairs={{0,12},{2,14},{4,0},{6,2},{8,4},{10,6},{12,8},{14,10},{1,13},{3,15... | collective-permute-start | bytes 3145736 | tf_op jit(solution)/shard_map/ppermute | solution.py:25
  79.3 4.1 %collective-permute-done.10.refs_7_ = f32[512,256]{1,0:T(8,128)S(1)} collective-permute-done((f32[512,256]{1,0:T(8,128)S(1)}, f32[512,256]{1,0:T(8,128)S(1)}, u32[]{:S(2)}, u32[]{:S(2)}) %collective-permute-start.10) | collective-permute-done | bytes 524320 | tf_op jit(solution)/shard_map/ppermute | solution.py:25
  83.4 11.2 %collective-permute-done.9.refs_6_ = f32[512,256]{1,0:T(8,128)S(1)} collective-permute-done((f32[512,256]{1,0:T(8,128)S(1)}, f32[512,256]{1,0:T(8,128)S(1)}, u32[]{:S(2)}, u32[]{:S(2)}) %collective-permute-start.9) | collective-permute-done | bytes 524320 | tf_op jit(solution)/shard_map/ppermute | solution.py:25
  94.7 11.1 %collective-permute-done.8.refs_5_ = f32[512,256]{1,0:T(8,128)S(1)} collective-permute-done((f32[512,256]{1,0:T(8,128)S(1)}, f32[512,256]{1,0:T(8,128)S(1)}, u32[]{:S(2)}, u32[]{:S(2)}) %collective-permute-start.8) | collective-permute-done | bytes 524320 | tf_op jit(solution)/shard_map/ppermute | solution.py:25
  105.8 2.2 %gram.10.mine = f32[264,256]{1,0:T(8,128)S(1)} custom-call(f32[256,512]{1,0:T(8,128)S(1)} %get-tuple-element.83.refs_0_, f32[256,512]{1,0:T(8,128)S(1)} %get-tuple-element.84.refs_1_, f32[256,512]{1,0:T(8,128)S(1)} %get-tuple-element.85.refs_2_, f32[256,512]{1,0:T(8,128)S(1)} %get-tuple-element.86.refs_3_, f32[512,256]{1,0:T(8,128)S(1)} %collective-permute-done.7.refs_4_, ...), custom_call_target="tpu_custom_call" | custom-call | flops 1024 | bytes 1024 | tf_op jit(solution)/shard_map/gram/pallas_call | solution.py:218
  108.1 1.5 collective-permute-done.11.other
  109.7 3.2 %rotation.9 = (bf16[512,256]{1,0:T(8,128)(2,1)S(1)}, bf16[512,256]{1,0:T(8,128)(2,1)S(1)}) custom-call(f32[20,256]{1,0:T(8,128)S(1)} %flags.1, f32[264,256]{1,0:T(8,128)S(1)} %gram.10.mine, f32[264,256]{1,0:T(8,128)S(1)} %collective-permute-done.11.other, f32[256,256]{1,0:T(8,128)S(1)} %add.9.refs_0_), custom_call_target="tpu_custom_call" | custom-call | flops 1024 | bytes 1024 | tf_op jit(solution)/shard_map/rotation/pallas_call | solution.py:312
  112.9 6.3 %rebuild.2 = (f32[2048,256]{1,0:T(8,128)S(1)}, f32[264,256]{1,0:T(8,128)S(1)}) custom-call(f32[512,256]{1,0:T(8,128)S(1)} %get-tuple-element.82.refs_0_, f32[512,256]{1,0:T(8,128)S(1)} %get-tuple-element.70.refs_1_, f32[512,256]{1,0:T(8,128)S(1)} %get-tuple-element.71.refs_2_, f32[512,256]{1,0:T(8,128)S(1)} %get-tuple-element.72.refs_3_, ...), custom_call_target="tpu_custom_call" | custom-call | flops 1024 | bytes 1024 | tf_op jit(solution)/shard_map/rebuild/pallas_call | solution.py:448
  119.7 1.4 collective-permute-done.13
  121.2 3.3 %rotation.10 = (bf16[512,512]{1,0:T(8,128)(2,1)S(1)}, bf16[512,512]{1,0:T(8,128)(2,1)S(1)}) custom-call(f32[20,256]{1,0:T(8,128)S(1)} %flags.1, f32[264,256]{1,0:T(8,128)S(1)} %get-tuple-element.92.mine, f32[264,256]{1,0:T(8,128)S(1)} %collective-permute-done.12.other, f32[256,256]{1,0:T(8,128)S(1)} %add.10.refs_0_), custom_call_target="tpu_custom_call" | custom-call | flops 1024 | bytes 1024 | tf_op jit(solution)/shard_map/rotation/pallas_call | solution.py:312
  124.5 7.0 %apply_all.3 = (f32[2048,256]{1,0:T(8,128)S(1)}, f32[256,2048]{1,0:T(8,128)}, f32[256,2048]{1,0:T(8,128)S(1)}, f32[256,256]{1,0:T(8,128)S(1)}, f32[1024,256]{1,0...) custom-call(f32[1024,256]{1,0:T(8,128)S(1)} %get-tuple-element.80.refs_0_, ...), custom_call_target="tpu_custom_call" | custom-call | flops 1024 | bytes 1024 | tf_op jit(solution)/shard_map/apply_all/pallas_call | solution.py:416
  131.5 1.5 collective-permute-start.20
  133.0 17.5 %collective-permute-done.15.refs_2_ = f32[1024,256]{1,0:T(8,128)S(1)} collective-permute-done((f32[1024,256]{1,0:T(8,128)S(1)}, f32[1024,256]{1,0:T(8,128)S(1)}, u32[]{:S(2)}, u32[]{:S(2)}) %collective-permute-start.15) | collective-permute-done | bytes 1048608 | tf_op jit(solution)/shard_map/ppermute | solution.py:25
  150.6 2.2 %gram.11.mine = f32[264,256]{1,0:T(8,128)S(1)} custom-call(f32[256,2048]{1,0:T(8,128)S(1)} %get-tuple-element.97.refs_0_, f32[1024,256]{1,0:T(8,128)S(1)} %collective-permute-done.14.refs_1_, f32[1024,256]{1,0:T(8,128)S(1)} %collective-permute-done.15.refs_2_, f32[256,256]{1,0:T(8,128)S(1)} %get-tuple-element.98.refs_3_), custom_call_target="tpu_custom_call" | custom-call | flops 1024 | bytes 1024 | tf_op jit(solution)/shard_map/gram/pallas_call | solution.py:218
  152.9 0.7 collective-permute-start.21
  153.6 0.8 collective-permute-done.16.other
  154.4 3.2 %rotation.11 = (bf16[512,256]{1,0:T(8,128)(2,1)S(1)}, bf16[512,256]{1,0:T(8,128)(2,1)S(1)}) custom-call(f32[20,256]{1,0:T(8,128)S(1)} %flags.1, f32[264,256]{1,0:T(8,128)S(1)} %gram.11.mine, f32[264,256]{1,0:T(8,128)S(1)} %collective-permute-done.16.other, f32[256,256]{1,0:T(8,128)S(1)} %add.10.refs_0_), custom_call_target="tpu_custom_call" | custom-call | flops 1024 | bytes 1024 | tf_op jit(solution)/shard_map/rotation/pallas_call | solution.py:312
  157.6 6.3 %rebuild.3 = (f32[2048,256]{1,0:T(8,128)S(1)}, f32[264,256]{1,0:T(8,128)S(1)}) custom-call(f32[2048,256]{1,0:T(8,128)S(1)} %get-tuple-element.96.refs_0_, f32[1024,256]{1,0:T(8,128)S(1)} %collective-permute-done.14.refs_1_, f32[1024,256]{1,0:T(8,128)S(1)} %collective-permute-done.15.refs_2_, bf16[512,256]{1,0:T(8,128)(2,1)S(1)} %get-tuple-element.99.refs_3_, ...), custom_call_target="tpu_custom_call" | custom-call | flops 1024 | bytes 1024 | tf_op jit(solution)/shard_map/rebuild/pallas_call | solution.py:448
  164.5 1.4 collective-permute-done.18
  165.9 3.3 %rotation.12 = (bf16[512,512]{1,0:T(8,128)(2,1)S(1)}, bf16[512,512]{1,0:T(8,128)(2,1)S(1)}, f32[136,256]{1,0:T(8,128)S(1)}) custom-call(f32[20,256]{1,0:T(8,128)S(1)} %flags.1, f32[264,256]{1,0:T(8,128)S(1)} %get-tuple-element.103.mine, f32[264,256]{1,0:T(8,128)S(1)} %collective-permute-done.17.other, f32[256,256]{1,0:T(8,128)S(1)} %add.11.refs_0_), custom_call_target="tpu_custom_call" | custom-call | flops 1024 | bytes 1024 | tf_op jit(solution)/shard_map/rotation/pallas_call | solution.py:312
  169.2 0.7 collective-permute-start.22
  170.0 0.8 apply_one.1.refs_0_
  170.7 2.6 %collective-permute-start.19 = (f32[512,256]{1,0:T(8,128)S(1)}, f32[512,256]{1,0:T(8,128)S(1)}, u32[]{:S(2)}, u32[]{:S(2)}) collective-permute-start(f32[512,256]{1,0:T(8,128)S(1)} %apply_one.1.refs_0_), channel_id=1, source_target_pairs={{0,4},{2,6},{4,8},{6,10},{8,12},{10,14},{12,0},{14,2},{1,5},{3,7},... | collective-permute-start | bytes 1572872 | tf_op jit(solution)/shard_map/ppermute | solution.py:25
  173.3 4.1 %finish.2 = (f32[2048,512]{1,0:T(8,128)}, f32[8,128]{1,0:T(8,128)S(1)}) custom-call(f32[20,256]{1,0:T(8,128)S(1)} %flags.1, f32[1024,256]{1,0:T(8,128)S(1)} %get-tuple-element.106.refs_0_, f32[512,256]{1,0:T(8,128)S(1)} %get-tuple-element.107.refs_1_, f32[512,256]{1,0:T(8,128)S(1)} %get-tuple-element.95.stay.refs_2_, ...), custom_call_target="tpu_custom_call" | custom-call | flops 1024 | bytes 1024 | tf_op jit(solution)/shard_map/finish/pallas_call | solution.py:563
  177.4 7.0 %collective-permute-done.21.refs_3_.refs_1_ = f32[512,256]{1,0:T(8,128)S(1)} collective-permute-done((f32[512,256]{1,0:T(8,128)S(1)}, f32[512,256]{1,0:T(8,128)S(1)}, u32[]{:S(2)}, u32[]{:S(2)}) %collective-permute-start.21) | collective-permute-done | bytes 524320 | tf_op jit(solution)/shard_map/ppermute | solution.py:25
  184.4 3.0 %collective-permute-done.22.message = f32[136,256]{1,0:T(8,128)S(1)} collective-permute-done((f32[136,256]{1,0:T(8,128)S(1)}, f32[136,256]{1,0:T(8,128)S(1)}, u32[]{:S(2)}, u32[]{:S(2)}) %collective-permute-start.22) | collective-permute-done | bytes 139296 | tf_op jit(solution)/shard_map/ppermute | solution.py:25
  187.5 1.3 collective-permute-done.23.other
  188.9 3.3 %rotation.13 = (bf16[512,256]{1,0:T(8,128)(2,1)S(1)}, bf16[512,256]{1,0:T(8,128)(2,1)S(1)}) custom-call(f32[20,256]{1,0:T(8,128)S(1)} %flags.1, f32[136,256]{1,0:T(8,128)S(1)} %relay.1.mine, f32[136,256]{1,0:T(8,128)S(1)} %collective-permute-done.23.other, f32[256,256]{1,0:T(8,128)S(1)} %add.11.refs_0_), custom_call_target="tpu_custom_call" | custom-call | flops 4000000000 | bytes 1024 | tf_op jit(solution)/shard_map/rotation/pallas_call | solution.py:312
  192.1 3.8 %finish.3 = (f32[2048,512]{1,0:T(8,128)}, f32[8,128]{1,0:T(8,128)}) custom-call(f32[20,256]{1,0:T(8,128)S(1)} %flags.1, f32[1024,256]{1,0:T(8,128)S(1)} %collective-permute-done.20.refs_2_.refs_0_, f32[512,256]{1,0:T(8,128)S(1)} %collective-permute-done.21.refs_3_.refs_1_, ...), custom_call_target="tpu_custom_call", output_to_operand_aliasing={{0}: (6, {})} | custom-call | flops 1024 | bytes 1024 | tf_op jit(solution)/shard_map/finish/pallas_call | solution.py:563
  195.9 2.0 collective-permute-done.19.came
  197.9 1.0 put.1
  (34 shorter events, 6.3 us)
Async XLA Ops:
  0.0 3.7 %copy-start = (s32[4,16]{1,0:T(4,128)S(1)}, s32[4,16]{1,0:T(4,128)}, u32[]{:S(2)}) copy-start(s32[4,16]{1,0:T(4,128)} %plan.1) | copy-start | bytes 772
  3.1 1.7 collective-permute-start
  8.8 17.6 %collective-permute-start.1 = (f32[512,256]{1,0:T(8,128)S(1)}, f32[512,256]{1,0:T(8,128)S(1)}, u32[]{:S(2)}, u32[]{:S(2)}) collective-permute-start(f32[512,256]{1,0:T(8,128)S(1)} %get-tuple-element.69), channel_id=1, source_target_pairs={{0,12},{2,14},{4,0},{6,2},{8,4},{10,6},{12,8},{14,10},{1,13},{3,15... | collective-permute-start | bytes 1572872 | tf_op jit(solution)/shard_map/ppermute | solution.py:25
  16.7 20.7 %collective-permute-start.2 = (f32[512,256]{1,0:T(8,128)S(1)}, f32[512,256]{1,0:T(8,128)S(1)}, u32[]{:S(2)}, u32[]{:S(2)}) collective-permute-start(f32[512,256]{1,0:T(8,128)S(1)} %get-tuple-element.70.refs_1_), channel_id=1, source_target_pairs={{0,12},{2,14},{4,0},{6,2},{8,4},{10,6},{12,8},{14,10},{1,13},{3,15... | collective-permute-start | bytes 1572872 | tf_op jit(solution)/shard_map/ppermute | solution.py:25
  20.1 28.6 %collective-permute-start.3 = (f32[512,256]{1,0:T(8,128)S(1)}, f32[512,256]{1,0:T(8,128)S(1)}, u32[]{:S(2)}, u32[]{:S(2)}) collective-permute-start(f32[512,256]{1,0:T(8,128)S(1)} %get-tuple-element.71.refs_2_), channel_id=1, source_target_pairs={{0,12},{2,14},{4,0},{6,2},{8,4},{10,6},{12,8},{14,10},{1,13},{3,15... | collective-permute-start | bytes 1572872 | tf_op jit(solution)/shard_map/ppermute | solution.py:25
  23.5 36.4 %collective-permute-start.4 = (f32[512,256]{1,0:T(8,128)S(1)}, f32[512,256]{1,0:T(8,128)S(1)}, u32[]{:S(2)}, u32[]{:S(2)}) collective-permute-start(f32[512,256]{1,0:T(8,128)S(1)} %get-tuple-element.72.refs_3_), channel_id=1, source_target_pairs={{0,12},{2,14},{4,0},{6,2},{8,4},{10,6},{12,8},{14,10},{1,13},{3,15... | collective-permute-start | bytes 1572872 | tf_op jit(solution)/shard_map/ppermute | solution.py:25
  26.4 35.8 %collective-permute-start.6 = (f32[256,256]{1,0:T(8,128)S(1)}, f32[256,256]{1,0:T(8,128)S(1)}, u32[]{:S(2)}, u32[]{:S(2)}) collective-permute-start(f32[256,256]{1,0:T(8,128)S(1)} %get-tuple-element.77), channel_id=1, source_target_pairs={{0,1},{1,0},{2,3},{3,2},{4,5},{5,4},{6,7},{7,6},{8,9},{9,8},{10,11... | collective-permute-start | bytes 786440 | tf_op jit(solution)/shard_map/ppermute | solution.py:25
  26.5 50.8 %collective-permute-start.7 = (f32[512,256]{1,0:T(8,128)S(1)}, f32[512,256]{1,0:T(8,128)S(1)}, u32[]{:S(2)}, u32[]{:S(2)}) collective-permute-start(f32[512,256]{1,0:T(8,128)S(1)} %get-tuple-element.65.refs_0_), channel_id=1, source_target_pairs={{0,4},{2,6},{4,8},{6,10},{8,12},{10,14},{12,0},{14,2},{1,5},{3,7},... | collective-permute-start | bytes 1572872 | tf_op jit(solution)/shard_map/ppermute | solution.py:25
  37.4 46.0 %collective-permute-start.10 = (f32[512,256]{1,0:T(8,128)S(1)}, f32[512,256]{1,0:T(8,128)S(1)}, u32[]{:S(2)}, u32[]{:S(2)}) collective-permute-start(f32[512,256]{1,0:T(8,128)S(1)} %get-tuple-element.68.refs_3_), channel_id=1, source_target_pairs={{0,4},{2,6},{4,8},{6,10},{8,12},{10,14},{12,0},{14,2},{1,5},{3,7},... | collective-permute-start | bytes 1572872 | tf_op jit(solution)/shard_map/ppermute | solution.py:25
  48.7 46.0 %collective-permute-start.9 = (f32[512,256]{1,0:T(8,128)S(1)}, f32[512,256]{1,0:T(8,128)S(1)}, u32[]{:S(2)}, u32[]{:S(2)}) collective-permute-start(f32[512,256]{1,0:T(8,128)S(1)} %get-tuple-element.67.refs_2_), channel_id=1, source_target_pairs={{0,4},{2,6},{4,8},{6,10},{8,12},{10,14},{12,0},{14,2},{1,5},{3,7},... | collective-permute-start | bytes 1572872 | tf_op jit(solution)/shard_map/ppermute | solution.py:25
  59.9 45.9 %collective-permute-start.8 = (f32[512,256]{1,0:T(8,128)S(1)}, f32[512,256]{1,0:T(8,128)S(1)}, u32[]{:S(2)}, u32[]{:S(2)}) collective-permute-start(f32[512,256]{1,0:T(8,128)S(1)} %get-tuple-element.66.refs_1_), channel_id=1, source_target_pairs={{0,4},{2,6},{4,8},{6,10},{8,12},{10,14},{12,0},{14,2},{1,5},{3,7},... | collective-permute-start | bytes 1572872 | tf_op jit(solution)/shard_map/ppermute | solution.py:25
  62.2 1.6 collective-permute-start.5
  73.0 60.1 %collective-permute-start.14 = (f32[1024,256]{1,0:T(8,128)S(1)}, f32[1024,256]{1,0:T(8,128)S(1)}, u32[]{:S(2)}, u32[]{:S(2)}) collective-permute-start(f32[1024,256]{1,0:T(8,128)S(1)} %get-tuple-element.80.refs_0_), channel_id=1, source_target_pairs={{0,12},{2,14},{4,0},{6,2},{8,4},{10,6},{12,8},{14,10},{1,13},{3,15... | collective-permute-start | bytes 3145736 | tf_op jit(solution)/shard_map/ppermute | solution.py:25
  77.3 73.3 %collective-permute-start.15 = (f32[1024,256]{1,0:T(8,128)S(1)}, f32[1024,256]{1,0:T(8,128)S(1)}, u32[]{:S(2)}, u32[]{:S(2)}) collective-permute-start(f32[1024,256]{1,0:T(8,128)S(1)} %get-tuple-element.81.refs_1_), channel_id=1, source_target_pairs={{0,12},{2,14},{4,0},{6,2},{8,4},{10,6},{12,8},{14,10},{1,13},{3,15... | collective-permute-start | bytes 3145736 | tf_op jit(solution)/shard_map/ppermute | solution.py:25
  108.0 1.6 collective-permute-start.11
  119.1 2.0 %collective-permute-start.12 = (f32[264,256]{1,0:T(8,128)S(1)}, f32[264,256]{1,0:T(8,128)S(1)}, u32[]{:S(2)}, u32[]{:S(2)}) collective-permute-start(f32[264,256]{1,0:T(8,128)S(1)} %get-tuple-element.92.mine), channel_id=1, source_target_pairs={{0,1},{1,0},{2,3},{3,2},{4,5},{5,4},{6,7},{7,6},{8,9},{9,8},{10,11... | collective-permute-start | bytes 811016 | tf_op jit(solution)/shard_map/ppermute | solution.py:25
  119.3 1.8 collective-permute-start.13
  131.5 53.0 %collective-permute-start.20 = (f32[1024,256]{1,0:T(8,128)S(1)}, f32[1024,256]{1,0:T(8,128)S(1)}, u32[]{:S(2)}, u32[]{:S(2)}) collective-permute-start(f32[1024,256]{1,0:T(8,128)S(1)} %get-tuple-element.106.refs_0_), channel_id=1, source_target_pairs={{0,4},{2,6},{4,8},{6,10},{8,12},{10,14},{12,0},{14,2},{1,5},{3,7},... | collective-permute-start | bytes 3145736 | tf_op jit(solution)/shard_map/ppermute | solution.py:25
  152.8 1.6 collective-permute-start.16
  152.9 31.6 %collective-permute-start.21 = (f32[512,256]{1,0:T(8,128)S(1)}, f32[512,256]{1,0:T(8,128)S(1)}, u32[]{:S(2)}, u32[]{:S(2)}) collective-permute-start(f32[512,256]{1,0:T(8,128)S(1)} %get-tuple-element.107.refs_1_), channel_id=1, source_target_pairs={{0,4},{2,6},{4,8},{6,10},{8,12},{10,14},{12,0},{14,2},{1,5},{3,7},... | collective-permute-start | bytes 1572872 | tf_op jit(solution)/shard_map/ppermute | solution.py:25
  163.9 2.0 %collective-permute-start.17 = (f32[264,256]{1,0:T(8,128)S(1)}, f32[264,256]{1,0:T(8,128)S(1)}, u32[]{:S(2)}, u32[]{:S(2)}) collective-permute-start(f32[264,256]{1,0:T(8,128)S(1)} %get-tuple-element.103.mine), channel_id=1, source_target_pairs={{0,1},{1,0},{2,3},{3,2},{4,5},{5,4},{6,7},{7,6},{8,9},{9,8},{10,11... | collective-permute-start | bytes 811016 | tf_op jit(solution)/shard_map/ppermute | solution.py:25
  164.1 1.8 collective-permute-start.18
  169.2 18.2 %collective-permute-start.22 = (f32[136,256]{1,0:T(8,128)S(1)}, f32[136,256]{1,0:T(8,128)S(1)}, u32[]{:S(2)}, u32[]{:S(2)}) collective-permute-start(f32[136,256]{1,0:T(8,128)S(1)} %get-tuple-element.109), channel_id=1, source_target_pairs={{0,4},{2,6},{4,8},{6,10},{8,12},{10,14},{12,0},{14,2},{1,5},{3,7},... | collective-permute-start | bytes 417800 | tf_op jit(solution)/shard_map/ppermute | solution.py:25
  170.7 27.1 %collective-permute-start.19 = (f32[512,256]{1,0:T(8,128)S(1)}, f32[512,256]{1,0:T(8,128)S(1)}, u32[]{:S(2)}, u32[]{:S(2)}) collective-permute-start(f32[512,256]{1,0:T(8,128)S(1)} %apply_one.1.refs_0_), channel_id=1, source_target_pairs={{0,4},{2,6},{4,8},{6,10},{8,12},{10,14},{12,0},{14,2},{1,5},{3,7},... | collective-permute-start | bytes 1572872 | tf_op jit(solution)/shard_map/ppermute | solution.py:25
  187.4 1.4 collective-permute-start.23

commit v3 on v2

--- a/solution.py
+++ b/solution.py
@@ -12,7 +12,7 @@
 BLOCK = 256
 PIECES = 4
 SIDE = 128
-PUT = 64
+PUT = 512
 GROUP = 4
 FIRST_MIB = 48
 PARAMS = pltpu.CompilerParams(vmem_limit_bytes=12 * 1024 * 1024)

time: 199 us -> 199 us (level)
  no operation moved by 1% of the time
where the time goes in v3:
time: 199 us
  waiting for transfers between devices  95 us (48%)
  Pallas kernels  80.4 us (40%)
  starting transfers between devices  22.9 us (12%)
    ppermute x24, waiting for transfers between devices, shift(): lax.ppermute(value, axis, [(i, (i + by) % size) for i in range(size)])  95 us
    pallas_call x7, Pallas kernels, rotation(): pl.pallas_call(functools.partial(rotation_kernel, step, side, both, note,...  23.6 us
    ppermute x24, starting transfers between devices, shift(): lax.ppermute(value, axis, [(i, (i + by) % size) for i in range(size)])  22.9 us
    pallas_call x2, Pallas kernels, apply_all(): pl.pallas_call(functools.partial(apply_all_kernel, (len(stay), len(move))...  12.8 us
    pallas_call x2, Pallas kernels, rebuild(): pl.pallas_call(functools.partial(rebuild_kernel, (len(sent), len(raw))),...  12.5 us
    pallas_call x4, Pallas kernels, apply_both(): pl.pallas_call(functools.partial(apply_both_kernel, first), grid=(blocks,...  11.4 us
    pallas_call x2, Pallas kernels, finish(): pl.pallas_call(functools.partial(finish_kernel, (len(stay), len(move)), k...  7.84 us
    pallas_call x6, Pallas kernels, gram(): pl.pallas_call(functools.partial(gram_kernel, (len(turned), len(came), le...  6.76 us
  transfers between devices with their start and end apart: 24, of which 17 were waited for; matrix products, arithmetic and copies ran while one was open for 0% of the time, Pallas kernels for 36%

profile of v3, /device:TPU:0, one launch (start us, length us, event | category | flops | bytes accessed | tf_op | source)
XLA Modules:
  0.0 198.9 jit_solution(11175746931353917140)
XLA Ops:
  0.0 3.1 %first_gram.1.mine = f32[272,256]{1,0:T(8,128)S(1)} custom-call(f32[2048,512]{1,0:T(8,128)} %joined.7), custom_call_target="tpu_custom_call" | custom-call | flops 1024 | bytes 1024 | tf_op jit(solution)/shard_map/first_gram/pallas_call | solution.py:149
  3.7 0.7 flags.1
  4.8 4.0 %rotation.7 = (bf16[512,512]{1,0:T(8,128)(2,1)S(1)}, bf16[512,512]{1,0:T(8,128)(2,1)S(1)}, f32[512,256]{1,0:T(8,128)S(1)}) custom-call(f32[20,256]{1,0:T(8,128)S(1)} %flags.1, f32[272,256]{1,0:T(8,128)S(1)} %first_gram.1.mine, f32[272,256]{1,0:T(8,128)S(1)} %collective-permute-done.other, f32[2048,512]{1,0:T(8,128)} %joined.7), custom_call_target="tpu_custom_call" | custom-call | flops 1024 | bytes 1024 | tf_op jit(solution)/shard_map/rotation/pallas_call | solution.py:312
  8.8 5.0 %collective-permute-start.1 = (f32[512,256]{1,0:T(8,128)S(1)}, f32[512,256]{1,0:T(8,128)S(1)}, u32[]{:S(2)}, u32[]{:S(2)}) collective-permute-start(f32[512,256]{1,0:T(8,128)S(1)} %get-tuple-element.69), channel_id=1, source_target_pairs={{0,12},{2,14},{4,0},{6,2},{8,4},{10,6},{12,8},{14,10},{1,13},{3,15... | collective-permute-start | bytes 1572872 | tf_op jit(solution)/shard_map/ppermute | solution.py:25
  13.9 2.8 %apply_both.4 = (f32[512,256]{1,0:T(8,128)S(1)}, f32[256,512]{1,0:T(8,128)S(1)}, f32[512,256]{1,0:T(8,128)S(1)}, f32[256,512]{1,0:T(8,128)S(1)}, f32[256,256]{1,0:T(8,128)S(1)}) custom-call(f32[2048,512]{1,0:T(8,128)} %joined.7, bf16[512,512]{1,0:T(8,128)(2,1)S(1)} %get-tuple-element.60.high, bf16[512,512]{1,0:T(8,128)(2,1)S(1)} %get-tuple-element.61.low), custom_call_target="tpu_custom_call" | custom-call | flops 1024 | bytes 1024 | tf_op jit(solution)/shard_map/apply_both/pallas_call | solution.py:363
  17.2 2.9 %apply_both.5 = (f32[512,256]{1,0:T(8,128)S(1)}, f32[256,512]{1,0:T(8,128)S(1)}, f32[512,256]{1,0:T(8,128)S(1)}, f32[256,512]{1,0:T(8,128)S(1)}, f32[256,256]{1,0:T(8,128)S(1)}) custom-call(f32[2048,512]{1,0:T(8,128)} %joined.7, bf16[512,512]{1,0:T(8,128)(2,1)S(1)} %get-tuple-element.60.high, bf16[512,512]{1,0:T(8,128)(2,1)S(1)} %get-tuple-element.61.low, ...), custom_call_target="tpu_custom_call" | custom-call | flops 1024 | bytes 1024 | tf_op jit(solution)/shard_map/apply_both/pallas_call | solution.py:363
  20.6 2.9 %apply_both.6 = (f32[512,256]{1,0:T(8,128)S(1)}, f32[256,512]{1,0:T(8,128)S(1)}, f32[512,256]{1,0:T(8,128)S(1)}, f32[256,512]{1,0:T(8,128)S(1)}, f32[256,256]{1,0:T(8,128)S(1)}) custom-call(f32[2048,512]{1,0:T(8,128)} %joined.7, bf16[512,512]{1,0:T(8,128)(2,1)S(1)} %get-tuple-element.60.high, bf16[512,512]{1,0:T(8,128)(2,1)S(1)} %get-tuple-element.61.low, ...), custom_call_target="tpu_custom_call" | custom-call | flops 1024 | bytes 1024 | tf_op jit(solution)/shard_map/apply_both/pallas_call | solution.py:363
  23.5 2.9 %apply_both.7 = (f32[512,256]{1,0:T(8,128)S(1)}, f32[256,512]{1,0:T(8,128)S(1)}, f32[512,256]{1,0:T(8,128)S(1)}, f32[256,512]{1,0:T(8,128)S(1)}, f32[256,256]{1,0:T(8,128)S(1)}) custom-call(f32[2048,512]{1,0:T(8,128)} %joined.7, bf16[512,512]{1,0:T(8,128)(2,1)S(1)} %get-tuple-element.60.high, bf16[512,512]{1,0:T(8,128)(2,1)S(1)} %get-tuple-element.61.low, ...), custom_call_target="tpu_custom_call" | custom-call | flops 1024 | bytes 1024 | tf_op jit(solution)/shard_map/apply_both/pallas_call | solution.py:363
  26.5 2.1 %collective-permute-start.7 = (f32[512,256]{1,0:T(8,128)S(1)}, f32[512,256]{1,0:T(8,128)S(1)}, u32[]{:S(2)}, u32[]{:S(2)}) collective-permute-start(f32[512,256]{1,0:T(8,128)S(1)} %get-tuple-element.65.refs_0_), channel_id=1, source_target_pairs={{0,4},{2,6},{4,8},{6,10},{8,12},{10,14},{12,0},{14,2},{1,5},{3,7},... | collective-permute-start | bytes 1572872 | tf_op jit(solution)/shard_map/ppermute | solution.py:25
  28.5 8.9 %collective-permute-done.2.refs_1_.refs_5_ = f32[512,256]{1,0:T(8,128)S(1)} collective-permute-done((f32[512,256]{1,0:T(8,128)S(1)}, f32[512,256]{1,0:T(8,128)S(1)}, u32[]{:S(2)}, u32[]{:S(2)}) %collective-permute-start.2) | collective-permute-done | bytes 524320 | tf_op jit(solution)/shard_map/ppermute | solution.py:25
  37.9 10.8 %collective-permute-done.3.refs_1_.refs_6_ = f32[512,256]{1,0:T(8,128)S(1)} collective-permute-done((f32[512,256]{1,0:T(8,128)S(1)}, f32[512,256]{1,0:T(8,128)S(1)}, u32[]{:S(2)}, u32[]{:S(2)}) %collective-permute-start.3) | collective-permute-done | bytes 524320 | tf_op jit(solution)/shard_map/ppermute | solution.py:25
  49.1 10.8 %collective-permute-done.4.refs_1_.refs_7_ = f32[512,256]{1,0:T(8,128)S(1)} collective-permute-done((f32[512,256]{1,0:T(8,128)S(1)}, f32[512,256]{1,0:T(8,128)S(1)}, u32[]{:S(2)}, u32[]{:S(2)}) %collective-permute-start.4) | collective-permute-done | bytes 524320 | tf_op jit(solution)/shard_map/ppermute | solution.py:25
  60.5 0.6 gram.7.refs_2_
  62.4 1.5 collective-permute-done.5.other
  63.9 3.3 %rotation.8 = (bf16[512,512]{1,0:T(8,128)(2,1)S(1)}, bf16[512,512]{1,0:T(8,128)(2,1)S(1)}) custom-call(f32[20,256]{1,0:T(8,128)S(1)} %flags.1, f32[264,256]{1,0:T(8,128)S(1)} %gram.9.mine, f32[264,256]{1,0:T(8,128)S(1)} %collective-permute-done.5.other, f32[256,256]{1,0:T(8,128)S(1)} %add.9.refs_0_), custom_call_target="tpu_custom_call" | custom-call | flops 1024 | bytes 1024 | tf_op jit(solution)/shard_map/rotation/pallas_call | solution.py:312
  67.1 5.8 %apply_all.2 = (f32[2048,256]{1,0:T(8,128)S(1)}, f32[256,2048]{1,0:T(8,128)S(1)}, f32[256,2048]{1,0:T(8,128)S(1)}, f32[256,256]{1,0:T(8,128)S(1)}, f32[1024,256]{1,0:T(8,128)S(1)}, /*index=5*/f32[1024,256]{1,0:T(8,128)S(1)}) custom-call(f32[512,256]{1,0:T(8,128)S(1)} %get-tuple-element.65.refs_0_, f32[512,256]{1,0:T(8,128)S(1)} %get-tuple-element.66.refs_1_, ...), custom_call_target="tpu_custom_call" | custom-call | flops 1024 | bytes 1024 | tf_op jit(solution)/shard_map/apply_all/pallas_call | solution.py:416
  73.0 4.3 %collective-permute-start.14 = (f32[1024,256]{1,0:T(8,128)S(1)}, f32[1024,256]{1,0:T(8,128)S(1)}, u32[]{:S(2)}, u32[]{:S(2)}) collective-permute-start(f32[1024,256]{1,0:T(8,128)S(1)} %get-tuple-element.80.refs_0_), channel_id=1, source_target_pairs={{0,12},{2,14},{4,0},{6,2},{8,4},{10,6},{12,8},{14,10},{1,13},{3,15... | collective-permute-start | bytes 3145736 | tf_op jit(solution)/shard_map/ppermute | solution.py:25
  77.3 2.0 %collective-permute-start.15 = (f32[1024,256]{1,0:T(8,128)S(1)}, f32[1024,256]{1,0:T(8,128)S(1)}, u32[]{:S(2)}, u32[]{:S(2)}) collective-permute-start(f32[1024,256]{1,0:T(8,128)S(1)} %get-tuple-element.81.refs_1_), channel_id=1, source_target_pairs={{0,12},{2,14},{4,0},{6,2},{8,4},{10,6},{12,8},{14,10},{1,13},{3,15... | collective-permute-start | bytes 3145736 | tf_op jit(solution)/shard_map/ppermute | solution.py:25
  79.3 4.1 %collective-permute-done.10.refs_7_ = f32[512,256]{1,0:T(8,128)S(1)} collective-permute-done((f32[512,256]{1,0:T(8,128)S(1)}, f32[512,256]{1,0:T(8,128)S(1)}, u32[]{:S(2)}, u32[]{:S(2)}) %collective-permute-start.10) | collective-permute-done | bytes 524320 | tf_op jit(solution)/shard_map/ppermute | solution.py:25
  83.4 11.2 %collective-permute-done.9.refs_6_ = f32[512,256]{1,0:T(8,128)S(1)} collective-permute-done((f32[512,256]{1,0:T(8,128)S(1)}, f32[512,256]{1,0:T(8,128)S(1)}, u32[]{:S(2)}, u32[]{:S(2)}) %collective-permute-start.9) | collective-permute-done | bytes 524320 | tf_op jit(solution)/shard_map/ppermute | solution.py:25
  94.7 11.1 %collective-permute-done.8.refs_5_ = f32[512,256]{1,0:T(8,128)S(1)} collective-permute-done((f32[512,256]{1,0:T(8,128)S(1)}, f32[512,256]{1,0:T(8,128)S(1)}, u32[]{:S(2)}, u32[]{:S(2)}) %collective-permute-start.8) | collective-permute-done | bytes 524320 | tf_op jit(solution)/shard_map/ppermute | solution.py:25
  105.8 2.2 %gram.10.mine = f32[264,256]{1,0:T(8,128)S(1)} custom-call(f32[256,512]{1,0:T(8,128)S(1)} %get-tuple-element.83.refs_0_, f32[256,512]{1,0:T(8,128)S(1)} %get-tuple-element.84.refs_1_, f32[256,512]{1,0:T(8,128)S(1)} %get-tuple-element.85.refs_2_, f32[256,512]{1,0:T(8,128)S(1)} %get-tuple-element.86.refs_3_, f32[512,256]{1,0:T(8,128)S(1)} %collective-permute-done.7.refs_4_, ...), custom_call_target="tpu_custom_call" | custom-call | flops 1024 | bytes 1024 | tf_op jit(solution)/shard_map/gram/pallas_call | solution.py:218
  108.1 1.5 collective-permute-done.11.other
  109.7 3.2 %rotation.9 = (bf16[512,256]{1,0:T(8,128)(2,1)S(1)}, bf16[512,256]{1,0:T(8,128)(2,1)S(1)}) custom-call(f32[20,256]{1,0:T(8,128)S(1)} %flags.1, f32[264,256]{1,0:T(8,128)S(1)} %gram.10.mine, f32[264,256]{1,0:T(8,128)S(1)} %collective-permute-done.11.other, f32[256,256]{1,0:T(8,128)S(1)} %add.9.refs_0_), custom_call_target="tpu_custom_call" | custom-call | flops 1024 | bytes 1024 | tf_op jit(solution)/shard_map/rotation/pallas_call | solution.py:312
  112.9 6.3 %rebuild.2 = (f32[2048,256]{1,0:T(8,128)S(1)}, f32[264,256]{1,0:T(8,128)S(1)}) custom-call(f32[512,256]{1,0:T(8,128)S(1)} %get-tuple-element.82.refs_0_, f32[512,256]{1,0:T(8,128)S(1)} %get-tuple-element.70.refs_1_, f32[512,256]{1,0:T(8,128)S(1)} %get-tuple-element.71.refs_2_, f32[512,256]{1,0:T(8,128)S(1)} %get-tuple-element.72.refs_3_, ...), custom_call_target="tpu_custom_call" | custom-call | flops 1024 | bytes 1024 | tf_op jit(solution)/shard_map/rebuild/pallas_call | solution.py:448
  119.7 1.4 collective-permute-done.13
  121.2 3.3 %rotation.10 = (bf16[512,512]{1,0:T(8,128)(2,1)S(1)}, bf16[512,512]{1,0:T(8,128)(2,1)S(1)}) custom-call(f32[20,256]{1,0:T(8,128)S(1)} %flags.1, f32[264,256]{1,0:T(8,128)S(1)} %get-tuple-element.92.mine, f32[264,256]{1,0:T(8,128)S(1)} %collective-permute-done.12.other, f32[256,256]{1,0:T(8,128)S(1)} %add.10.refs_0_), custom_call_target="tpu_custom_call" | custom-call | flops 1024 | bytes 1024 | tf_op jit(solution)/shard_map/rotation/pallas_call | solution.py:312
  124.5 7.0 %apply_all.3 = (f32[2048,256]{1,0:T(8,128)S(1)}, f32[256,2048]{1,0:T(8,128)}, f32[256,2048]{1,0:T(8,128)S(1)}, f32[256,256]{1,0:T(8,128)S(1)}, f32[1024,256]{1,0...) custom-call(f32[1024,256]{1,0:T(8,128)S(1)} %get-tuple-element.80.refs_0_, ...), custom_call_target="tpu_custom_call" | custom-call | flops 1024 | bytes 1024 | tf_op jit(solution)/shard_map/apply_all/pallas_call | solution.py:416
  131.5 1.5 collective-permute-start.20
  133.0 17.5 %collective-permute-done.15.refs_2_ = f32[1024,256]{1,0:T(8,128)S(1)} collective-permute-done((f32[1024,256]{1,0:T(8,128)S(1)}, f32[1024,256]{1,0:T(8,128)S(1)}, u32[]{:S(2)}, u32[]{:S(2)}) %collective-permute-start.15) | collective-permute-done | bytes 1048608 | tf_op jit(solution)/shard_map/ppermute | solution.py:25
  150.6 2.2 %gram.11.mine = f32[264,256]{1,0:T(8,128)S(1)} custom-call(f32[256,2048]{1,0:T(8,128)S(1)} %get-tuple-element.97.refs_0_, f32[1024,256]{1,0:T(8,128)S(1)} %collective-permute-done.14.refs_1_, f32[1024,256]{1,0:T(8,128)S(1)} %collective-permute-done.15.refs_2_, f32[256,256]{1,0:T(8,128)S(1)} %get-tuple-element.98.refs_3_), custom_call_target="tpu_custom_call" | custom-call | flops 1024 | bytes 1024 | tf_op jit(solution)/shard_map/gram/pallas_call | solution.py:218
  152.9 0.7 collective-permute-start.21
  153.6 0.8 collective-permute-done.16.other
  154.4 3.2 %rotation.11 = (bf16[512,256]{1,0:T(8,128)(2,1)S(1)}, bf16[512,256]{1,0:T(8,128)(2,1)S(1)}) custom-call(f32[20,256]{1,0:T(8,128)S(1)} %flags.1, f32[264,256]{1,0:T(8,128)S(1)} %gram.11.mine, f32[264,256]{1,0:T(8,128)S(1)} %collective-permute-done.16.other, f32[256,256]{1,0:T(8,128)S(1)} %add.10.refs_0_), custom_call_target="tpu_custom_call" | custom-call | flops 1024 | bytes 1024 | tf_op jit(solution)/shard_map/rotation/pallas_call | solution.py:312
  157.6 6.3 %rebuild.3 = (f32[2048,256]{1,0:T(8,128)S(1)}, f32[264,256]{1,0:T(8,128)S(1)}) custom-call(f32[2048,256]{1,0:T(8,128)S(1)} %get-tuple-element.96.refs_0_, f32[1024,256]{1,0:T(8,128)S(1)} %collective-permute-done.14.refs_1_, f32[1024,256]{1,0:T(8,128)S(1)} %collective-permute-done.15.refs_2_, bf16[512,256]{1,0:T(8,128)(2,1)S(1)} %get-tuple-element.99.refs_3_, ...), custom_call_target="tpu_custom_call" | custom-call | flops 1024 | bytes 1024 | tf_op jit(solution)/shard_map/rebuild/pallas_call | solution.py:448
  164.5 1.4 collective-permute-done.18
  165.9 3.3 %rotation.12 = (bf16[512,512]{1,0:T(8,128)(2,1)S(1)}, bf16[512,512]{1,0:T(8,128)(2,1)S(1)}, f32[136,256]{1,0:T(8,128)S(1)}) custom-call(f32[20,256]{1,0:T(8,128)S(1)} %flags.1, f32[264,256]{1,0:T(8,128)S(1)} %get-tuple-element.103.mine, f32[264,256]{1,0:T(8,128)S(1)} %collective-permute-done.17.other, f32[256,256]{1,0:T(8,128)S(1)} %add.11.refs_0_), custom_call_target="tpu_custom_call" | custom-call | flops 1024 | bytes 1024 | tf_op jit(solution)/shard_map/rotation/pallas_call | solution.py:312
  169.2 0.7 collective-permute-start.22
  170.0 0.8 apply_one.1.refs_0_
  170.7 2.6 %collective-permute-start.19 = (f32[512,256]{1,0:T(8,128)S(1)}, f32[512,256]{1,0:T(8,128)S(1)}, u32[]{:S(2)}, u32[]{:S(2)}) collective-permute-start(f32[512,256]{1,0:T(8,128)S(1)} %apply_one.1.refs_0_), channel_id=1, source_target_pairs={{0,4},{2,6},{4,8},{6,10},{8,12},{10,14},{12,0},{14,2},{1,5},{3,7},... | collective-permute-start | bytes 1572872 | tf_op jit(solution)/shard_map/ppermute | solution.py:25
  173.3 4.1 %finish.2 = (f32[2048,512]{1,0:T(8,128)}, f32[8,128]{1,0:T(8,128)S(1)}) custom-call(f32[20,256]{1,0:T(8,128)S(1)} %flags.1, f32[1024,256]{1,0:T(8,128)S(1)} %get-tuple-element.106.refs_0_, f32[512,256]{1,0:T(8,128)S(1)} %get-tuple-element.107.refs_1_, f32[512,256]{1,0:T(8,128)S(1)} %get-tuple-element.95.stay.refs_2_, ...), custom_call_target="tpu_custom_call" | custom-call | flops 1024 | bytes 1024 | tf_op jit(solution)/shard_map/finish/pallas_call | solution.py:563
  177.4 7.0 %collective-permute-done.21.refs_3_.refs_1_ = f32[512,256]{1,0:T(8,128)S(1)} collective-permute-done((f32[512,256]{1,0:T(8,128)S(1)}, f32[512,256]{1,0:T(8,128)S(1)}, u32[]{:S(2)}, u32[]{:S(2)}) %collective-permute-start.21) | collective-permute-done | bytes 524320 | tf_op jit(solution)/shard_map/ppermute | solution.py:25
  184.4 3.0 %collective-permute-done.22.message = f32[136,256]{1,0:T(8,128)S(1)} collective-permute-done((f32[136,256]{1,0:T(8,128)S(1)}, f32[136,256]{1,0:T(8,128)S(1)}, u32[]{:S(2)}, u32[]{:S(2)}) %collective-permute-start.22) | collective-permute-done | bytes 139296 | tf_op jit(solution)/shard_map/ppermute | solution.py:25
  187.5 1.3 collective-permute-done.23.other
  188.9 3.3 %rotation.13 = (bf16[512,256]{1,0:T(8,128)(2,1)S(1)}, bf16[512,256]{1,0:T(8,128)(2,1)S(1)}) custom-call(f32[20,256]{1,0:T(8,128)S(1)} %flags.1, f32[136,256]{1,0:T(8,128)S(1)} %relay.1.mine, f32[136,256]{1,0:T(8,128)S(1)} %collective-permute-done.23.other, f32[256,256]{1,0:T(8,128)S(1)} %add.11.refs_0_), custom_call_target="tpu_custom_call" | custom-call | flops 4000000000 | bytes 1024 | tf_op jit(solution)/shard_map/rotation/pallas_call | solution.py:312
  192.1 3.8 %finish.3 = (f32[2048,512]{1,0:T(8,128)}, f32[8,128]{1,0:T(8,128)}) custom-call(f32[20,256]{1,0:T(8,128)S(1)} %flags.1, f32[1024,256]{1,0:T(8,128)S(1)} %collective-permute-done.20.refs_2_.refs_0_, f32[512,256]{1,0:T(8,128)S(1)} %collective-permute-done.21.refs_3_.refs_1_, ...), custom_call_target="tpu_custom_call", output_to_operand_aliasing={{0}: (6, {})} | custom-call | flops 1024 | bytes 1024 | tf_op jit(solution)/shard_map/finish/pallas_call | solution.py:563
  195.9 2.0 collective-permute-done.19.came
  197.9 0.9 put.1
  (34 shorter events, 6.3 us)
Async XLA Ops:
  0.0 3.7 %copy-start = (s32[4,16]{1,0:T(4,128)S(1)}, s32[4,16]{1,0:T(4,128)}, u32[]{:S(2)}) copy-start(s32[4,16]{1,0:T(4,128)} %plan.1) | copy-start | bytes 772
  3.1 1.7 collective-permute-start
  8.8 17.6 %collective-permute-start.1 = (f32[512,256]{1,0:T(8,128)S(1)}, f32[512,256]{1,0:T(8,128)S(1)}, u32[]{:S(2)}, u32[]{:S(2)}) collective-permute-start(f32[512,256]{1,0:T(8,128)S(1)} %get-tuple-element.69), channel_id=1, source_target_pairs={{0,12},{2,14},{4,0},{6,2},{8,4},{10,6},{12,8},{14,10},{1,13},{3,15... | collective-permute-start | bytes 1572872 | tf_op jit(solution)/shard_map/ppermute | solution.py:25
  16.7 20.7 %collective-permute-start.2 = (f32[512,256]{1,0:T(8,128)S(1)}, f32[512,256]{1,0:T(8,128)S(1)}, u32[]{:S(2)}, u32[]{:S(2)}) collective-permute-start(f32[512,256]{1,0:T(8,128)S(1)} %get-tuple-element.70.refs_1_), channel_id=1, source_target_pairs={{0,12},{2,14},{4,0},{6,2},{8,4},{10,6},{12,8},{14,10},{1,13},{3,15... | collective-permute-start | bytes 1572872 | tf_op jit(solution)/shard_map/ppermute | solution.py:25
  20.1 28.6 %collective-permute-start.3 = (f32[512,256]{1,0:T(8,128)S(1)}, f32[512,256]{1,0:T(8,128)S(1)}, u32[]{:S(2)}, u32[]{:S(2)}) collective-permute-start(f32[512,256]{1,0:T(8,128)S(1)} %get-tuple-element.71.refs_2_), channel_id=1, source_target_pairs={{0,12},{2,14},{4,0},{6,2},{8,4},{10,6},{12,8},{14,10},{1,13},{3,15... | collective-permute-start | bytes 1572872 | tf_op jit(solution)/shard_map/ppermute | solution.py:25
  23.5 36.4 %collective-permute-start.4 = (f32[512,256]{1,0:T(8,128)S(1)}, f32[512,256]{1,0:T(8,128)S(1)}, u32[]{:S(2)}, u32[]{:S(2)}) collective-permute-start(f32[512,256]{1,0:T(8,128)S(1)} %get-tuple-element.72.refs_3_), channel_id=1, source_target_pairs={{0,12},{2,14},{4,0},{6,2},{8,4},{10,6},{12,8},{14,10},{1,13},{3,15... | collective-permute-start | bytes 1572872 | tf_op jit(solution)/shard_map/ppermute | solution.py:25
  26.4 35.8 %collective-permute-start.6 = (f32[256,256]{1,0:T(8,128)S(1)}, f32[256,256]{1,0:T(8,128)S(1)}, u32[]{:S(2)}, u32[]{:S(2)}) collective-permute-start(f32[256,256]{1,0:T(8,128)S(1)} %get-tuple-element.77), channel_id=1, source_target_pairs={{0,1},{1,0},{2,3},{3,2},{4,5},{5,4},{6,7},{7,6},{8,9},{9,8},{10,11... | collective-permute-start | bytes 786440 | tf_op jit(solution)/shard_map/ppermute | solution.py:25
  26.5 50.8 %collective-permute-start.7 = (f32[512,256]{1,0:T(8,128)S(1)}, f32[512,256]{1,0:T(8,128)S(1)}, u32[]{:S(2)}, u32[]{:S(2)}) collective-permute-start(f32[512,256]{1,0:T(8,128)S(1)} %get-tuple-element.65.refs_0_), channel_id=1, source_target_pairs={{0,4},{2,6},{4,8},{6,10},{8,12},{10,14},{12,0},{14,2},{1,5},{3,7},... | collective-permute-start | bytes 1572872 | tf_op jit(solution)/shard_map/ppermute | solution.py:25
  37.4 46.0 %collective-permute-start.10 = (f32[512,256]{1,0:T(8,128)S(1)}, f32[512,256]{1,0:T(8,128)S(1)}, u32[]{:S(2)}, u32[]{:S(2)}) collective-permute-start(f32[512,256]{1,0:T(8,128)S(1)} %get-tuple-element.68.refs_3_), channel_id=1, source_target_pairs={{0,4},{2,6},{4,8},{6,10},{8,12},{10,14},{12,0},{14,2},{1,5},{3,7},... | collective-permute-start | bytes 1572872 | tf_op jit(solution)/shard_map/ppermute | solution.py:25
  48.7 46.0 %collective-permute-start.9 = (f32[512,256]{1,0:T(8,128)S(1)}, f32[512,256]{1,0:T(8,128)S(1)}, u32[]{:S(2)}, u32[]{:S(2)}) collective-permute-start(f32[512,256]{1,0:T(8,128)S(1)} %get-tuple-element.67.refs_2_), channel_id=1, source_target_pairs={{0,4},{2,6},{4,8},{6,10},{8,12},{10,14},{12,0},{14,2},{1,5},{3,7},... | collective-permute-start | bytes 1572872 | tf_op jit(solution)/shard_map/ppermute | solution.py:25
  59.9 45.9 %collective-permute-start.8 = (f32[512,256]{1,0:T(8,128)S(1)}, f32[512,256]{1,0:T(8,128)S(1)}, u32[]{:S(2)}, u32[]{:S(2)}) collective-permute-start(f32[512,256]{1,0:T(8,128)S(1)} %get-tuple-element.66.refs_1_), channel_id=1, source_target_pairs={{0,4},{2,6},{4,8},{6,10},{8,12},{10,14},{12,0},{14,2},{1,5},{3,7},... | collective-permute-start | bytes 1572872 | tf_op jit(solution)/shard_map/ppermute | solution.py:25
  62.2 1.6 collective-permute-start.5
  73.0 60.1 %collective-permute-start.14 = (f32[1024,256]{1,0:T(8,128)S(1)}, f32[1024,256]{1,0:T(8,128)S(1)}, u32[]{:S(2)}, u32[]{:S(2)}) collective-permute-start(f32[1024,256]{1,0:T(8,128)S(1)} %get-tuple-element.80.refs_0_), channel_id=1, source_target_pairs={{0,12},{2,14},{4,0},{6,2},{8,4},{10,6},{12,8},{14,10},{1,13},{3,15... | collective-permute-start | bytes 3145736 | tf_op jit(solution)/shard_map/ppermute | solution.py:25
  77.3 73.3 %collective-permute-start.15 = (f32[1024,256]{1,0:T(8,128)S(1)}, f32[1024,256]{1,0:T(8,128)S(1)}, u32[]{:S(2)}, u32[]{:S(2)}) collective-permute-start(f32[1024,256]{1,0:T(8,128)S(1)} %get-tuple-element.81.refs_1_), channel_id=1, source_target_pairs={{0,12},{2,14},{4,0},{6,2},{8,4},{10,6},{12,8},{14,10},{1,13},{3,15... | collective-permute-start | bytes 3145736 | tf_op jit(solution)/shard_map/ppermute | solution.py:25
  108.0 1.6 collective-permute-start.11
  119.1 2.0 %collective-permute-start.12 = (f32[264,256]{1,0:T(8,128)S(1)}, f32[264,256]{1,0:T(8,128)S(1)}, u32[]{:S(2)}, u32[]{:S(2)}) collective-permute-start(f32[264,256]{1,0:T(8,128)S(1)} %get-tuple-element.92.mine), channel_id=1, source_target_pairs={{0,1},{1,0},{2,3},{3,2},{4,5},{5,4},{6,7},{7,6},{8,9},{9,8},{10,11... | collective-permute-start | bytes 811016 | tf_op jit(solution)/shard_map/ppermute | solution.py:25
  119.3 1.8 collective-permute-start.13
  131.5 53.0 %collective-permute-start.20 = (f32[1024,256]{1,0:T(8,128)S(1)}, f32[1024,256]{1,0:T(8,128)S(1)}, u32[]{:S(2)}, u32[]{:S(2)}) collective-permute-start(f32[1024,256]{1,0:T(8,128)S(1)} %get-tuple-element.106.refs_0_), channel_id=1, source_target_pairs={{0,4},{2,6},{4,8},{6,10},{8,12},{10,14},{12,0},{14,2},{1,5},{3,7},... | collective-permute-start | bytes 3145736 | tf_op jit(solution)/shard_map/ppermute | solution.py:25
  152.8 1.6 collective-permute-start.16
  152.9 31.6 %collective-permute-start.21 = (f32[512,256]{1,0:T(8,128)S(1)}, f32[512,256]{1,0:T(8,128)S(1)}, u32[]{:S(2)}, u32[]{:S(2)}) collective-permute-start(f32[512,256]{1,0:T(8,128)S(1)} %get-tuple-element.107.refs_1_), channel_id=1, source_target_pairs={{0,4},{2,6},{4,8},{6,10},{8,12},{10,14},{12,0},{14,2},{1,5},{3,7},... | collective-permute-start | bytes 1572872 | tf_op jit(solution)/shard_map/ppermute | solution.py:25
  163.9 2.0 %collective-permute-start.17 = (f32[264,256]{1,0:T(8,128)S(1)}, f32[264,256]{1,0:T(8,128)S(1)}, u32[]{:S(2)}, u32[]{:S(2)}) collective-permute-start(f32[264,256]{1,0:T(8,128)S(1)} %get-tuple-element.103.mine), channel_id=1, source_target_pairs={{0,1},{1,0},{2,3},{3,2},{4,5},{5,4},{6,7},{7,6},{8,9},{9,8},{10,11... | collective-permute-start | bytes 811016 | tf_op jit(solution)/shard_map/ppermute | solution.py:25
  164.1 1.8 collective-permute-start.18
  169.2 18.2 %collective-permute-start.22 = (f32[136,256]{1,0:T(8,128)S(1)}, f32[136,256]{1,0:T(8,128)S(1)}, u32[]{:S(2)}, u32[]{:S(2)}) collective-permute-start(f32[136,256]{1,0:T(8,128)S(1)} %get-tuple-element.109), channel_id=1, source_target_pairs={{0,4},{2,6},{4,8},{6,10},{8,12},{10,14},{12,0},{14,2},{1,5},{3,7},... | collective-permute-start | bytes 417800 | tf_op jit(solution)/shard_map/ppermute | solution.py:25
  170.7 27.1 %collective-permute-start.19 = (f32[512,256]{1,0:T(8,128)S(1)}, f32[512,256]{1,0:T(8,128)S(1)}, u32[]{:S(2)}, u32[]{:S(2)}) collective-permute-start(f32[512,256]{1,0:T(8,128)S(1)} %apply_one.1.refs_0_), channel_id=1, source_target_pairs={{0,4},{2,6},{4,8},{6,10},{8,12},{10,14},{12,0},{14,2},{1,5},{3,7},... | collective-permute-start | bytes 1572872 | tf_op jit(solution)/shard_map/ppermute | solution.py:25
  187.4 1.4 collective-permute-start.23
